TPU v7x, 512 devices: a whole 4x8x8 slice. The times are simulated.
512 devices in a mesh: island: 4 (over z_hi), section: 16 (over y, z_lo), fsdp: 8 (over x, core).
Axes of the slice: x: 4, y: 8, z: 8 (z_hi: 4, z_lo: 2; z = z_hi * 2 + z_lo), core: 2. Of those that a mesh axis runs over, the one named last changes fastest.
Arguments:
- hidden: bfloat16 [4, 16, 1024, 4096], P('island', 'section', 'fsdp'), may hold values from -6 to 6
- norm_gain: float32 [16, 4096], P('section'), may hold values from 0.1 to 1.9
- key_grad: bfloat16 [4, 16, 1024, 512], P('island', 'section', 'fsdp'), may hold values from -18 to 18
- local_weight: bfloat16 [4, 16, 4096, 512], P('island', 'section', 'fsdp'), may hold values from -0.09375 to 0.09375
- drift: float32 [4, 16, 4096, 512], P('island', 'section', 'fsdp'), may hold values from -6 to 6
- momentum: float32 [16, 256, 4096], P('section', 'island', 'fsdp'), may hold values from -12 to 12
- seeds: int32 [16], P('section'), may hold values from 0 to 999999
Outputs:
- input_grad: bfloat16 [4, 16, 1024, 4096], P('island', 'section', 'fsdp')
- new_momentum: float32 [16, 256, 4096], P('section', 'island', 'fsdp')
- outer_update: float32 [16, 4096, 512], P('section', 'fsdp')
All inputs are finite; a program needn't handle non-finite values.
Results may differ from a plain program's by a relative error of at most 0.014.
Values may be sent and summed in bfloat16 or wider, within the bound.
No kernel may reach another device: no remote copies, remote signals or barrier semaphores. Data moves between devices by JAX's collectives and lax.ppermute only.
A program may use at most 128 MiB of HBM per device.

v0:
```python
import math

import jax
import jax.numpy as jnp
from jax import lax
from jax.sharding import PartitionSpec as P

RANK = 256


inner_rate = 0.01
outer_rate = 0.7
momentum_rate = 0.9


def carried_in(part, axis, combine, identity):
    count = lax.axis_size(axis)
    place = lax.axis_index(axis)
    ahead = count - 1 - place
    gathered = lax.all_gather(part, axis)
    state = jnp.zeros_like(part) + jnp.asarray(identity, part.dtype)

    def one(lap, state):
        source = count - 1 - lap
        return combine(state, lax.dynamic_index_in_dim(gathered, source, 0, False))

    return lax.fori_loop(0, ahead, one, state)


def projection_basis(seed_value, row_count, column_count):
    row_index = lax.broadcasted_iota(jnp.int32, (row_count, column_count), 0)
    column_index = lax.broadcasted_iota(jnp.int32, (row_count, column_count), 1)
    hashed = row_index * column_count + column_index + seed_value * 7919
    hashed = hashed * 1664525 + 1013904223 & 2147483647
    hashed = hashed ^ hashed >> 15
    hashed = hashed * 1103515245 + 12345 & 2147483647
    hashed = hashed ^ hashed >> 13
    levels = (hashed & 65535).astype(jnp.float32)
    return (levels - 32767.5) * (math.sqrt(12.0 / column_count) / 65536.0)


def add_terms(earlier, later):
    return earlier + later


def shards(hidden, norm_gain, key_grad, local_weight, drift, momentum, seeds):
    values = hidden[0, 0].astype(jnp.float32)
    gain_row = norm_gain[0]
    section_keys = key_grad[0, 0]
    weight_part = local_weight[0, 0]
    key_width = weight_part.shape[1]
    recip = lax.rsqrt(jnp.mean(values * values, -1, keepdims=True) + 1e-05)
    unit = values * recip
    normed = (unit * gain_row).astype(jnp.bfloat16)
    key_back = lax.dot_general(
        section_keys,
        lax.all_gather(weight_part, "fsdp", axis=0, tiled=True),
        (((1,), (1,)), ((), ())),
        preferred_element_type=jnp.float32,
    )
    weight_grad = lax.psum_scatter(
        lax.dot_general(
            normed, section_keys, (((0,), (0,)), ((), ())), preferred_element_type=jnp.float32
        ).astype(jnp.bfloat16),
        "fsdp",
        scatter_dimension=0,
        tiled=True,
    ).astype(jnp.float32)
    scaled = gain_row * key_back
    branch = recip * (scaled - unit * jnp.mean(scaled * unit, -1, keepdims=True))
    later_sum = carried_in(branch, "section", add_terms, jnp.zeros_like(branch))
    input_grad = (branch + later_sum).astype(jnp.bfloat16)
    delta = drift[0, 0] + inner_rate * weight_grad
    basis_row = projection_basis(seeds[0], key_width, RANK)
    factor = jnp.einsum("kr,dk->rd", basis_row, delta, precision=lax.Precision.HIGHEST)
    total_factor = lax.psum(factor.astype(jnp.bfloat16), "island").astype(jnp.float32)
    mean_factor = total_factor / lax.axis_size("island")
    rank_share = momentum.shape[1]
    island_place = lax.axis_index("island")
    own_factor = lax.dynamic_slice_in_dim(mean_factor, island_place * rank_share, rank_share, 0)
    momentum_part = momentum_rate * momentum[0] + own_factor
    step_part = own_factor + momentum_rate * momentum_part
    step_factor = lax.all_gather(step_part, "island", axis=0, tiled=True)
    outer_update = outer_rate * jnp.einsum(
        "rd,kr->dk", step_factor, basis_row, precision=lax.Precision.HIGHEST
    )
    return (input_grad[None, None], momentum_part[None], outer_update[None])


def solution(mesh):
    return jax.shard_map(
        shards,
        mesh=mesh,
        in_specs=(
            P("island", "section", "fsdp", None),
            P("section", None),
            P("island", "section", "fsdp", None),
            P("island", "section", "fsdp", None),
            P("island", "section", "fsdp", None),
            P("section", "island", "fsdp"),
            P("section"),
        ),
        out_specs=(
            P("island", "section", "fsdp", None),
            P("section", "island", "fsdp"),
            P("section", "fsdp", None),
        ),
        check_vma=False,
    )
```

profile of v0, /device:TPU:1, one launch (start us, length us, event | category | flops | bytes accessed | tf_op | source)
XLA Modules:
  0.0 894.1 jit_solution(10822899487937764192)
XLA Ops:
  9.5 4.1 convolution_convert_fusion
  14.3 39.2 %all-gather.5.cloned.1.call-done = bf16[1,1,4096,512]{3,2,1,0:T(8,128)(2,1)} async-done(((bf16[1,1,512,512]{3,2,1,0:T(8,128)(2,1)}), bf16[1,1,4096,512]{3,2,1,0:T(8,128)(2,1)}) %all-gather.5.cloned.1.call-update) | async-done | bytes 4194320 | tf_op jit(solution)/shard_map/all_gather | solution.py:57
  53.6 3.8 fusion.5
  57.3 39.7 %reduce-scatter.2.cloned.1.call-done = bf16[512,512]{1,0:T(8,128)(2,1)} async-done(((bf16[4096,512]{1,0:T(8,128)(2,1)}), bf16[512,512]{1,0:T(8,128)(2,1)}) %reduce-scatter.2.cloned.1.call-update) | async-done | bytes 524304 | tf_op jit(solution)/shard_map/reduce_scatter | solution.py:61
  97.0 4.2 convolution_convert_fusion.1
  103.2 54.9 %all-reduce.2.cloned.1.call-done = bf16[256,512]{1,0:T(8,128)(2,1)} async-done(((bf16[256,512]{1,0:T(8,128)(2,1)}), bf16[256,512]{1,0:T(8,128)(2,1)}) %all-reduce.2.cloned.1.call-update) | async-done | bytes 262160 | tf_op jit(solution)/shard_map/psum | solution.py:76
  159.6 14.1 %all_gather.15 = f32[256,512]{1,0:T(8,128)S(1)} all-gather(f32[64,512]{1,0:T(8,128)S(1)} %get-tuple-element.68), channel_id=1, replica_groups=mesh['island'=4,'section'=16,'fsdp'=8] {'island'}, dimensions={0}, use_global_device_ids=true | all-gather | bytes 655360 | tf_op jit(solution)/shard_map/all_gather | solution.py:83
  173.8 3.1 fusion.11
  176.9 675.7 %all-gather.7.cloned.1.call-done = f32[2048,4096]{1,0:T(8,128)} async-done(((f32[128,4096]{1,0:T(8,128)}), f32[2048,4096]{1,0:T(8,128)}) %all-gather.7.cloned.1.call-update) | async-done | bytes 33554448 | tf_op jit(solution)/shard_map/all_gather | solution.py:20
  852.8 32.1 %while.12 = (s32[]{:T(128)}, f32[128,4096]{1,0:T(8,128)S(1)}, s32[]{:T(128)}, f32[16,128,4096]{2,1,0:T(8,128)}, s32[]{:T(128)}, /*index=5*/s32[]{:T(128)}, s32[]{:T(128)}, s32[]{:T(128)}) while((s32[]{:T(128)}, f32[128,4096]{1,0:T(8,128)S(1)}, s32[]{:T(128)}, f32[16,128,4096]{2,1,0:T(8,128)}, s32[]{:T(128)}, /*index=5*/s32[]{:T(128)}, ...), condition=%wide.region_3.4_spmd, body=%wide.region_2.0_spmd.sunk | while | flops 524294 | bytes 6291591 | solution.py:27
  852.8 2.1 bitcast_add_fusion.5
  854.9 2.1 bitcast_add_fusion.5
  857.1 2.1 bitcast_add_fusion.5
  859.2 2.1 bitcast_add_fusion.5
  861.3 2.1 bitcast_add_fusion.5
  863.5 2.1 bitcast_add_fusion.5
  865.6 2.1 bitcast_add_fusion.5
  867.8 2.1 bitcast_add_fusion.5
  872.0 2.1 bitcast_add_fusion.5
  874.2 2.1 bitcast_add_fusion.5
  878.4 2.1 bitcast_add_fusion.5
  880.6 2.1 bitcast_add_fusion.5
  882.7 2.1 bitcast_add_fusion.5
  884.8 2.8 fusion.12
  (25 shorter events, 10.2 us)
Async XLA Ops:
  7.2 2.3 copy-start
  7.2 2.3 copy-start.1
  7.2 46.4 %all-gather.5.cloned.1.call-start = ((), (), s32[]{:S(2)}) async-start(), calls=%async_computation.3 | async-start | bytes 4718592 | tf_op jit(solution)/shard_map/all_gather | solution.py:57
  7.9 89.1 %reduce-scatter.2.cloned.1.call-start = ((), (), s32[]{:S(2)}) async-start(), calls=%async_computation.1 | async-start | bytes 4718592 | tf_op jit(solution)/shard_map/reduce_scatter | solution.py:61
  13.6 40.0 %copy-start.2 = (f32[1,4096]{1,0:T(1,128)S(1)}, f32[1,4096]{1,0:T(1,128)}, u32[]{:S(2)}) copy-start(f32[1,4096]{1,0:T(1,128)} %param.10) | copy-start | bytes 49156
  13.6 144.5 %all-reduce.2.cloned.1.call-start = ((), (), s32[]{:S(2)}) async-start(), calls=%async_computation.2 | async-start | bytes 524288 | tf_op jit(solution)/shard_map/psum | solution.py:76
  101.3 751.3 %all-gather.7.cloned.1.call-start = ((), (), s32[]{:S(2)}) async-start(), calls=%async_computation.4 | async-start | bytes 35651584 | tf_op jit(solution)/shard_map/all_gather | solution.py:20
  103.1 55.0 %copy-start.3 = (f32[1,64,512]{2,1,0:T(8,128)S(1)}, f32[1,64,512]{2,1,0:T(8,128)}, u32[]{:S(2)}) copy-start(f32[1,64,512]{2,1,0:T(8,128)} %param.14) | copy-start | bytes 393220
Sparse Core Ops, SparseCore 0:
  10.2 43.3 all-gather.4
  56.4 40.5 reduce-scatter.1
  101.4 56.6 all-reduce.1
  160.2 692.2 all-gather.6
where the time goes:
time: 895 us; the launch traced here: 894 us
  waiting for transfers between devices  810 us (91%)
  other arithmetic  39.3 us (4%)
  matrix products  15.2 us (2%)
  between operations  14.5 us (2%)
  blocking collectives  14.1 us (2%)
    all_gather x1, waiting for transfers between devices, carried_in(): gathered = lax.all_gather(part, axis)  676 us
    psum x1, waiting for transfers between devices, shards(): lax.psum(factor.astype(jnp.bfloat16), 'island').astype(jnp.float32)  54.9 us
    reduce_scatter x1, waiting for transfers between devices, shards(): lax.psum_scatter(lax.dot_general(normed, section_keys, (((0,), (0,)), (()...  39.7 us
    all_gather x1, waiting for transfers between devices, shards(): lax.all_gather(weight_part, 'fsdp', axis=0, tiled=True)  39.2 us
    add x15, other arithmetic, add_terms(): return earlier + later  31.7 us
  transfers between devices with their start and end apart: 4, of which 4 were waited for; matrix products, arithmetic and copies ran while one was open for 2% of the time, Pallas kernels for 0%

commit v1 on v0

v1 whole, which is shorter than its diff:
```python
import math

import jax
import jax.numpy as jnp
from jax import lax
from jax.experimental import pallas as pl
from jax.experimental.pallas import tpu as pltpu
from jax.sharding import PartitionSpec as P

RANK = 256


inner_rate = 0.01
outer_rate = 0.7
momentum_rate = 0.9


def projection_basis(seed_value, row_count, column_count):
    row_index = lax.broadcasted_iota(jnp.int32, (row_count, column_count), 0)
    column_index = lax.broadcasted_iota(jnp.int32, (row_count, column_count), 1)
    hashed = row_index * column_count + column_index + seed_value * 7919
    hashed = hashed * 1664525 + 1013904223 & 2147483647
    hashed = hashed ^ hashed >> 15
    hashed = hashed * 1103515245 + 12345 & 2147483647
    hashed = hashed ^ hashed >> 13
    levels = (hashed & 65535).astype(jnp.float32)
    return (levels - 32767.5) * (math.sqrt(12.0 / column_count) / 65536.0)


def suffix_kernel(parts_ref, sums_ref):
    count, _, width = parts_ref.shape
    step = 512

    def chunk(place, carry):
        span = pl.ds(pl.multiple_of(place * step, step), step)
        total = parts_ref[count - 1, :, span].astype(jnp.float32)
        sums_ref[count - 1, :, span] = total.astype(sums_ref.dtype)
        for source in range(count - 2, -1, -1):
            total = total + parts_ref[source, :, span].astype(jnp.float32)
            sums_ref[source, :, span] = total.astype(sums_ref.dtype)
        return carry

    lax.fori_loop(0, width // step, chunk, 0)


def suffix_sums(parts):
    return pl.pallas_call(
        suffix_kernel,
        out_shape=jax.ShapeDtypeStruct(parts.shape, parts.dtype),
        in_specs=[pl.BlockSpec(memory_space=pltpu.VMEM)],
        out_specs=pl.BlockSpec(memory_space=pltpu.VMEM),
        compiler_params=pltpu.CompilerParams(vmem_limit_bytes=16 * 1024 * 1024),
        name="suffix_sums",
    )(parts)


def shards(hidden, norm_gain, key_grad, local_weight, drift, momentum, seeds):
    tokens, width = hidden.shape[2:]
    sections = lax.axis_size("section")
    islands = lax.axis_size("island")
    weight = lax.all_gather(local_weight[0, 0], "fsdp", axis=0, tiled=True)
    values = hidden[0, 0].astype(jnp.float32)
    gain_row = norm_gain[0]
    section_keys = key_grad[0, 0]
    key_width = section_keys.shape[1]
    recip = lax.rsqrt(jnp.mean(values * values, -1, keepdims=True) + 1e-05)
    unit = values * recip
    normed = (unit * gain_row).astype(jnp.bfloat16)

    basis_row = projection_basis(seeds[0], key_width, RANK)
    projected_keys = jnp.dot(
        section_keys.astype(jnp.float32), basis_row, precision=lax.Precision.HIGHEST
    ).astype(jnp.bfloat16)
    partial_factor = lax.dot_general(
        projected_keys, normed, (((0,), (0,)), ((), ())), preferred_element_type=jnp.float32
    ).astype(jnp.bfloat16)
    drift_factor = jnp.einsum("kr,dk->rd", basis_row, drift[0, 0], precision=lax.Precision.HIGHEST)
    all_momentum = lax.all_gather(momentum[0], "island", axis=0, tiled=True)

    key_back = lax.dot_general(
        section_keys, weight, (((1,), (1,)), ((), ())), preferred_element_type=jnp.float32
    )
    scaled = gain_row * key_back
    branch = recip * (scaled - unit * jnp.mean(scaled * unit, -1, keepdims=True))
    pieces = branch.astype(jnp.bfloat16).reshape(sections, tokens // sections, width)
    pieces = lax.all_to_all(pieces, "section", 0, 0)
    pieces = lax.all_to_all(suffix_sums(pieces), "section", 0, 0)
    input_grad = pieces.reshape(tokens, width)

    gradient_factor = lax.psum_scatter(partial_factor, "fsdp", scatter_dimension=1, tiled=True)
    factor = drift_factor + inner_rate * gradient_factor.astype(jnp.float32)
    total_factor = lax.psum(factor.astype(jnp.bfloat16), "island").astype(jnp.float32)
    mean_factor = total_factor / islands
    next_momentum = momentum_rate * all_momentum + mean_factor
    step_factor = mean_factor + momentum_rate * next_momentum
    rank_share = momentum.shape[1]
    own_momentum = lax.dynamic_slice_in_dim(
        next_momentum, lax.axis_index("island") * rank_share, rank_share, 0
    )
    outer_update = outer_rate * jnp.einsum(
        "rd,kr->dk", step_factor, basis_row, precision=lax.Precision.HIGHEST
    )
    return (input_grad[None, None], own_momentum[None], outer_update[None])


def solution(mesh):
    return jax.shard_map(
        shards,
        mesh=mesh,
        in_specs=(
            P("island", "section", "fsdp", None),
            P("section", None),
            P("island", "section", "fsdp", None),
            P("island", "section", "fsdp", None),
            P("island", "section", "fsdp", None),
            P("section", "island", "fsdp"),
            P("section"),
        ),
        out_specs=(
            P("island", "section", "fsdp", None),
            P("section", "island", "fsdp"),
            P("section", "fsdp", None),
        ),
        check_vma=False,
    )
```

time: 895 us -> 177 us (0.20)
  the two profiles are of different devices: /device:TPU:1 before, /device:TPU:2 now
where the time goes in v1:
time: 177 us
  waiting for transfers between devices  69.9 us (39%)
  blocking collectives  66.8 us (38%)
  matrix products  15.6 us (9%)
  between operations  14.5 us (8%)
  starting transfers between devices  3.91 us (2%)
  other arithmetic  3.08 us (2%)
    all_gather x1, waiting for transfers between devices, shards(): weight = lax.all_gather(local_weight[0, 0], 'fsdp', axis=0, tiled=True)  37.2 us
    all_to_all x1, blocking collectives, shards(): pieces = lax.all_to_all(pieces, 'section', 0, 0)  37 us
    psum x1, waiting for transfers between devices, shards(): lax.psum(factor.astype(jnp.bfloat16), 'island').astype(jnp.float32)  32 us
    all_gather x1, blocking collectives, shards(): all_momentum = lax.all_gather(momentum[0], 'island', axis=0, tiled=True)  29.8 us
    dot_general x1, matrix products, shards(): jnp.einsum('rd,kr->dk', step_factor, basis_row, precision=lax.Precision.H...  4.14 us
    all_to_all x1, starting transfers between devices, shards(): pieces = lax.all_to_all(suffix_sums(pieces), 'section', 0, 0)  3.79 us
    dot_general x1, matrix products, shards(): lax.dot_general(section_keys, weight, (((1,), (1,)), ((), ())), preferred...  3.78 us
    dot_general x1, matrix products, shards(): jnp.einsum('kr,dk->rd', basis_row, drift[0, 0], precision=lax.Precision.H...  3.76 us
  transfers between devices with their start and end apart: 4, of which 2 were waited for; matrix products, arithmetic and copies ran while one was open for 11% of the time, Pallas kernels for 1%

profile of v1, /device:TPU:2, one launch (start us, length us, event | category | flops | bytes accessed | tf_op | source)
XLA Modules:
  0.0 176.6 jit_solution(8366026095497661995)
XLA Ops:
  7.2 0.0 copy-start
  7.2 0.0 all-gather.4.cloned.1.call-start
  7.2 0.7 all-gather.4.cloned.1.call-update
  7.9 0.0 reduce-scatter.2.cloned.1.call-start
  8.6 1.5 fusion.9
  10.2 1.8 %convolution_convert_fusion.1 = bf16[256,128]{1,0:T(8,128)(2,1)S(1)} fusion(s32[]{:T(128)} %bitcast.8, s32[512]{0:T(512)S(1)} %iota_multiply_fusion, bf16[1,1,128,512]{3,2,1,0:T(8,128)(2,1)} %param.9), kind=kOutput, calls=%fused_computation.18 | convolution fusion | flops 203456512 | bytes 198660 | tf_op jit(solution)/shard_map/dot_general | solution.py:71
  12.0 2.1 %convolution_convert_fusion = bf16[256,4096]{1,0:T(8,128)(2,1)} fusion(bf16[256,128]{1,0:T(8,128)(2,1)S(1)} %convolution_convert_fusion.1, bf16[1,1,128,4096]{3,2,1,0:T(8,128)(2,1)S(1)} %copy-done.1, f32[4096]{0:T(1024)S(1)} %bitcast.40, f32[128]{0:T(128)S(1)} %add_rsqrt_fusion), kind=kOutput, calls=%fused_computation | convolution fusion | flops 271581184 | bytes 3228160 | tf_op jit(solution)/shard_map/dot_general | solution.py:74
  14.1 0.0 reduce-scatter.2.cloned.1.call-update
  14.1 37.2 %all-gather.4.cloned.1.call-done = bf16[1,1,4096,512]{3,2,1,0:T(8,128)(2,1)} async-done(((bf16[1,1,512,512]{3,2,1,0:T(8,128)(2,1)}), bf16[1,1,4096,512]{3,2,1,0:T(8,128)(2,1)}) %all-gather.4.cloned.1.call-update) | async-done | bytes 4194320 | tf_op jit(solution)/shard_map/all_gather | solution.py:61
  51.3 3.8 %fusion.4 = (f32[128]{0:T(128)S(1)}, f32[128,4096]{1,0:T(8,128)S(1)}) fusion(bf16[1,1,128,4096]{3,2,1,0:T(8,128)(2,1)S(1)} %copy-done.1, f32[128]{0:T(128)S(1)} %add_rsqrt_fusion, bf16[1,1,4096,512]{3,2,1,0:T(8,128)(2,1)} %all-gather.4.cloned.1.call-done, bf16[1,1,128,512]{3,2,1,0:T(8,128)(2,1)S(1)} %copy-done.2, f32[4096]{0:T(1024)S(1)} %bitcast.41), kind=kOutput, calls=%fused_computation.8 | convolution fusion | flops 539492224 | bytes 7488512 | tf_op jit(solution)/shard_map/dot_general | solution.py:80
  55.1 0.5 fusion.13
  55.6 37.0 %all_to_all.10.parts_ref = bf16[16,8,4096]{2,1,0:T(8,128)(2,1)S(1)} all-to-all(bf16[16,8,4096]{2,1,0:T(8,128)(2,1)S(1)} %fusion.13), channel_id=1, replica_groups=mesh['island'=4,'section'=16,'fsdp'=8] {'section'}, dimensions={0} | all-to-all | bytes 2097152 | tf_op jit(solution)/shard_map/all_to_all | solution.py:86
  92.6 1.2 suffix_sums.1
  93.8 3.8 %all-to-all-start.1 = ((bf16[16,8,4096]{2,1,0:T(8,128)(2,1)}), bf16[16,8,4096]{2,1,0:T(8,128)(2,1)S(1)}, u32[]{:S(2)}, u32[]{:S(2)}) async-start(bf16[16,8,4096]{2,1,0:T(8,128)(2,1)} %suffix_sums.1), calls=%async_computation.1 | async-start | bytes 2097152 | tf_op jit(solution)/shard_map/all_to_all | solution.py:87
  97.6 0.0 all-reduce.2.cloned.1.call-start
  97.7 0.0 reduce-scatter.2.cloned.1.call-done
  97.7 3.8 %fusion.11 = bf16[256,512]{1,0:T(8,128)(2,1)} fusion(f32[1,1,512,512]{3,2,1,0:T(8,128)S(1)} %copy-done, bf16[256,512]{1,0:T(8,128)(2,1)} %reduce-scatter.2.cloned.1.call-done, s32[]{:T(128)} %bitcast.8, s32[512]{0:T(512)S(1)} %iota_multiply_fusion), kind=kOutput, calls=%fused_computation.17 | convolution fusion | flops 807927808 | bytes 1574916 | tf_op jit(solution)/shard_map/kr,dk->rd/dot_general | solution.py:77
  101.5 0.0 all-reduce.2.cloned.1.call-update
  101.5 29.8 %all-gather.1 = f32[1,256,512]{2,1,0:T(8,128)S(1)} all-gather(f32[1,64,512]{2,1,0:T(8,128)S(1)} %copy-done.3), channel_id=3, replica_groups=mesh['island'=4,'section'=16,'fsdp'=8] {'island'}, dimensions={1}, use_global_device_ids=true | all-gather | bytes 655360 | tf_op jit(solution)/shard_map/all_gather | solution.py:78
  131.2 32.0 %all-reduce.2.cloned.1.call-done = bf16[256,512]{1,0:T(8,128)(2,1)} async-done(((bf16[256,512]{1,0:T(8,128)(2,1)}), bf16[256,512]{1,0:T(8,128)(2,1)}) %all-reduce.2.cloned.1.call-update) | async-done | bytes 262160 | tf_op jit(solution)/shard_map/psum | solution.py:92
  163.3 1.0 bitcast_add_fusion
  164.3 0.7 dynamic-slice_bitcast_fusion
  165.0 4.1 %fusion.10 = f32[1,512,512]{2,1,0:T(8,128)} fusion(bf16[256,512]{1,0:T(8,128)(2,1)} %all-reduce.2.cloned.1.call-done, s32[]{:T(128)} %bitcast.8, s32[512]{0:T(512)S(1)} %iota_multiply_fusion, f32[1,256,512]{2,1,0:T(8,128)S(1)} %all-gather.1), kind=kOutput, calls=%fused_computation.15 | convolution fusion | flops 808452096 | bytes 1837060 | tf_op jit(solution)/shard_map/rd,kr->dk/dot_general | solution.py:100
  169.1 1.0 copy.13
  (13 shorter events, 0.0 us)
Async XLA Ops:
  7.2 90.5 %copy-start = (f32[1,1,512,512]{3,2,1,0:T(8,128)S(1)}, f32[1,1,512,512]{3,2,1,0:T(8,128)}, u32[]{:S(2)}) copy-start(f32[1,1,512,512]{3,2,1,0:T(8,128)} %param.11) | copy-start | bytes 3145732
  7.2 4.8 %copy-start.1 = (bf16[1,1,128,4096]{3,2,1,0:T(8,128)(2,1)S(1)}, bf16[1,1,128,4096]{3,2,1,0:T(8,128)(2,1)}, u32[]{:S(2)}) copy-start(bf16[1,1,128,4096]{3,2,1,0:T(8,128)(2,1)} %param.7) | copy-start | bytes 3145732
  7.2 4.8 %copy-start.4 = (f32[1,4096]{1,0:T(1,128)S(1)}, f32[1,4096]{1,0:T(1,128)}, u32[]{:S(2)}) copy-start(f32[1,4096]{1,0:T(1,128)} %param.8) | copy-start | bytes 49156
  7.2 44.1 %all-gather.4.cloned.1.call-start = ((), (), s32[]{:S(2)}) async-start(), calls=%async_computation.5 | async-start | bytes 4718592 | tf_op jit(solution)/shard_map/all_gather | solution.py:61
  7.9 89.7 %reduce-scatter.2.cloned.1.call-start = ((), (), s32[]{:S(2)}) async-start(), calls=%async_computation.3 | async-start | bytes 2359296 | tf_op jit(solution)/shard_map/reduce_scatter | solution.py:90
  12.0 39.3 %copy-start.2 = (bf16[1,1,128,512]{3,2,1,0:T(8,128)(2,1)S(1)}, bf16[1,1,128,512]{3,2,1,0:T(8,128)(2,1)}, u32[]{:S(2)}) copy-start(bf16[1,1,128,512]{3,2,1,0:T(8,128)(2,1)} %param.9) | copy-start | bytes 393220
  93.8 7.7 %copy-start.3 = (f32[1,64,512]{2,1,0:T(8,128)S(1)}, f32[1,64,512]{2,1,0:T(8,128)}, u32[]{:S(2)}) copy-start(f32[1,64,512]{2,1,0:T(8,128)} %param.12) | copy-start | bytes 393220
  93.8 75.3 %all-to-all-start.1 = ((bf16[16,8,4096]{2,1,0:T(8,128)(2,1)}), bf16[16,8,4096]{2,1,0:T(8,128)(2,1)S(1)}, u32[]{:S(2)}, u32[]{:S(2)}) async-start(bf16[16,8,4096]{2,1,0:T(8,128)(2,1)} %suffix_sums.1), calls=%async_computation.1 | async-start | bytes 2097152 | tf_op jit(solution)/shard_map/all_to_all | solution.py:87
  97.6 65.7 %all-reduce.2.cloned.1.call-start = ((), (), s32[]{:S(2)}) async-start(), calls=%async_computation.4 | async-start | bytes 524288 | tf_op jit(solution)/shard_map/psum | solution.py:92
Sparse Core Ops, SparseCore 0:
  10.2 41.0 all-gather.3
  54.1 37.0 reduce-scatter.1
  101.9 61.2 all-reduce.1

commit v2 on v1

v2 whole, which is shorter than its diff:
```python
import math

import jax
import jax.numpy as jnp
from jax import lax
from jax.experimental import pallas as pl
from jax.experimental.pallas import tpu as pltpu
from jax.sharding import PartitionSpec as P

RANK = 256
CORES = 2


inner_rate = 0.01
outer_rate = 0.7
momentum_rate = 0.9


def projection_basis(seed_value, row_count, column_count):
    row_index = lax.broadcasted_iota(jnp.int32, (row_count, column_count), 0)
    column_index = lax.broadcasted_iota(jnp.int32, (row_count, column_count), 1)
    hashed = row_index * column_count + column_index + seed_value * 7919
    hashed = hashed * 1664525 + 1013904223 & 2147483647
    hashed = hashed ^ hashed >> 15
    hashed = hashed * 1103515245 + 12345 & 2147483647
    hashed = hashed ^ hashed >> 13
    levels = (hashed & 65535).astype(jnp.float32)
    return (levels - 32767.5) * (math.sqrt(12.0 / column_count) / 65536.0)


def whole_vmem():
    return pl.BlockSpec(memory_space=pltpu.VMEM)


def whole_hbm():
    return pl.BlockSpec(memory_space=pltpu.HBM)


def in_hbm(array):
    return pltpu.with_memory_space_constraint(array, pltpu.HBM)


def kernel_params():
    return pltpu.CompilerParams(vmem_limit_bytes=24 * 1024 * 1024)


def suffix_kernel(parts_ref, sums_ref, out, out_sems):
    chunks, count, _, step = out.shape

    def departure(place):
        span = pl.ds(place * step, step)
        return pltpu.make_async_copy(out.at[place], sums_ref.at[:, :, span], out_sems.at[place])

    for place in range(chunks):
        span = pl.ds(place * step, step)
        total = parts_ref[count - 1, :, span].astype(jnp.float32)
        out[place, count - 1] = total.astype(out.dtype)
        for source in range(count - 2, -1, -1):
            total = total + parts_ref[source, :, span].astype(jnp.float32)
            out[place, source] = total.astype(out.dtype)
        departure(place).start()
    for place in range(chunks):
        departure(place).wait()


def suffix_sums(parts):
    count, rows, width = parts.shape
    step = 512
    chunks = width // step
    return pl.pallas_call(
        suffix_kernel,
        out_shape=pltpu.HBM(parts.shape, parts.dtype),
        in_specs=[whole_vmem()],
        out_specs=whole_hbm(),
        scratch_shapes=[
            pltpu.VMEM((chunks, count, rows, step), parts.dtype),
            pltpu.SemaphoreType.DMA((chunks,)),
        ],
        compiler_params=kernel_params(),
        name="suffix_sums",
    )(pltpu.with_memory_space_constraint(parts, pltpu.VMEM))


def key_back_kernel(
    core_ref, keys_ref, own_ref, other_ref, back_ref, held, out, held_sem, out_sems
):
    chips = keys_ref.shape[0]
    width = own_ref.shape[0]
    core = core_ref[0]
    arrival = pltpu.make_async_copy(other_ref.at[pl.ds(0, width)], held, held_sem)
    arrival.start()

    def departure(chip):
        return pltpu.make_async_copy(out.at[chip], back_ref.at[chip], out_sems.at[chip])

    for weight_ref, place in ((own_ref, core), (held, 1 - core)):
        span = pl.ds(pl.multiple_of(place * width, width), width)
        if weight_ref is held:
            arrival.wait()
        for chip in range(chips):
            out[chip, :, span] = lax.dot_general(
                keys_ref[chip],
                weight_ref[...],
                (((1,), (1,)), ((), ())),
                preferred_element_type=jnp.float32,
            ).astype(out.dtype)
            if weight_ref is held:
                departure(chip).start()
    for chip in range(chips):
        departure(chip).wait()


def key_back_columns(core, keys, own_weight, arrived):
    chips, tokens, _ = keys.shape
    shape = (chips, tokens, CORES * own_weight.shape[0])
    return pl.pallas_call(
        key_back_kernel,
        out_shape=pltpu.HBM(shape, jnp.bfloat16),
        in_specs=[pl.BlockSpec(memory_space=pltpu.SMEM), whole_vmem(), whole_vmem(), whole_hbm()],
        out_specs=whole_hbm(),
        scratch_shapes=[
            pltpu.VMEM(own_weight.shape, own_weight.dtype),
            pltpu.VMEM(shape, jnp.bfloat16),
            pltpu.SemaphoreType.DMA,
            pltpu.SemaphoreType.DMA((chips,)),
        ],
        compiler_params=kernel_params(),
        name="key_back_columns",
    )(core.reshape(1), keys, own_weight, in_hbm(arrived))


def prepare_kernel(
    core_ref,
    hidden_ref,
    gain_ref,
    weight_ref,
    own_ref,
    swap_ref,
    held,
    own_out,
    swap_out,
    weight,
    held_sems,
    own_sems,
    swap_sems,
):
    tokens, width = hidden_ref.shape
    chips, _, slice_width = own_ref.shape
    chunks = held_sems.shape[0] - 1
    core = core_ref[0]
    rows = 16
    each = tokens // chunks

    def arrival(chunk):
        lines = pl.ds(chunk * each, each)
        return pltpu.make_async_copy(hidden_ref.at[lines], held.at[lines], held_sems.at[chunk])

    weight_in = pltpu.make_async_copy(weight_ref, weight, held_sems.at[chunks])
    weight_out = pltpu.make_async_copy(
        weight, swap_ref.at[pl.ds(0, slice_width)], swap_sems.at[chips]
    )
    for chunk in range(chunks):
        arrival(chunk).start()
    weight_in.start()

    def group(place, carry):
        lines = pl.ds(pl.multiple_of(place * rows, rows), rows)
        squares = jnp.zeros((rows, 128), jnp.float32)
        for at in range(0, width, 128):
            value = held[lines, at : at + 128].astype(jnp.float32)
            squares = squares + value * value
        recip = lax.rsqrt(jnp.sum(squares, -1, keepdims=True) / width + 1e-05)

        def normed(chip, side):
            at = pl.multiple_of((CORES * chip + side) * slice_width, slice_width)
            span = pl.ds(at, slice_width)
            value = held[lines, span].astype(jnp.float32) * recip
            return (value * gain_ref[:, span]).astype(own_out.dtype)

        for chip in range(chips):
            own_out[chip, lines, :] = normed(chip, core)
            swap_out[chip, lines, :] = normed(chip, 1 - core)
        return carry

    for chunk in range(chunks):
        arrival(chunk).wait()
        lax.fori_loop(chunk * each // rows, (chunk + 1) * each // rows, group, 0)
        if chunk == 0:
            weight_in.wait()
            weight_out.start()

    def departures(chip):
        at = slice_width + chip * tokens
        return (
            pltpu.make_async_copy(
                swap_out.at[chip], swap_ref.at[pl.ds(at, tokens)], swap_sems.at[chip]
            ),
            pltpu.make_async_copy(own_out.at[chip], own_ref.at[chip], own_sems.at[chip]),
        )

    for chip in range(chips):
        for copy in departures(chip):
            copy.start()
    weight_out.wait()
    for chip in range(chips):
        for copy in departures(chip):
            copy.wait()


def prepare(core, hidden, gain_row, weight):
    tokens, width = hidden.shape
    slice_width, key_width = weight.shape
    chips = width // slice_width // CORES
    chunks = 4
    columns = (chips, tokens, slice_width)
    return pl.pallas_call(
        prepare_kernel,
        out_shape=(
            pltpu.HBM(columns, jnp.bfloat16),
            pltpu.HBM((slice_width + chips * tokens, key_width), jnp.bfloat16),
        ),
        in_specs=[
            pl.BlockSpec(memory_space=pltpu.SMEM),
            whole_hbm(),
            whole_vmem(),
            whole_hbm(),
        ],
        out_specs=(whole_hbm(),) * 2,
        scratch_shapes=[
            pltpu.VMEM(hidden.shape, hidden.dtype),
            pltpu.VMEM(columns, jnp.bfloat16),
            pltpu.VMEM(columns, jnp.bfloat16),
            pltpu.VMEM(weight.shape, weight.dtype),
            pltpu.SemaphoreType.DMA((chunks + 1,)),
            pltpu.SemaphoreType.DMA((chips,)),
            pltpu.SemaphoreType.DMA((chips + 1,)),
        ],
        compiler_params=kernel_params(),
        name="prepare",
    )(core.reshape(1), in_hbm(hidden), gain_row, in_hbm(weight))


def pair_kernel(chip_ref, own_ref, other_ref, *refs):
    part_refs, (held, in_sems, out_sems) = refs[:-3], refs[-3:]
    chips, tokens, _ = own_ref.shape
    first = other_ref.shape[0] - chips * tokens
    arrivals, departures = [], []
    for turn, part_ref in enumerate(part_refs):
        target = lax.rem(chip_ref[0] + turn, chips)
        lines = pl.ds(pl.multiple_of(first + target * tokens, tokens), tokens)
        for side, source in enumerate((own_ref.at[target], other_ref.at[lines])):
            place = held.at[turn, side]
            arrivals.append(pltpu.make_async_copy(source, place, in_sems.at[turn, side]))
            departures.append(
                pltpu.make_async_copy(place, part_ref.at[side], out_sems.at[turn, side])
            )
    for copy in arrivals:
        copy.start()
    for arrival, departure in zip(arrivals, departures, strict=True):
        arrival.wait()
        departure.start()
    for copy in departures:
        copy.wait()


def pair_columns(chip, own_normed, arrived):
    chips, tokens, slice_width = own_normed.shape
    shape = (CORES, tokens, slice_width)
    return pl.pallas_call(
        pair_kernel,
        out_shape=(pltpu.HBM(shape, own_normed.dtype),) * chips,
        in_specs=[pl.BlockSpec(memory_space=pltpu.SMEM)] + [whole_hbm()] * 2,
        out_specs=(whole_hbm(),) * chips,
        scratch_shapes=[
            pltpu.VMEM((chips, *shape), own_normed.dtype),
            pltpu.SemaphoreType.DMA((chips, CORES)),
            pltpu.SemaphoreType.DMA((chips, CORES)),
        ],
        compiler_params=kernel_params(),
        name="pair_columns",
    )(chip.reshape(1), in_hbm(own_normed), in_hbm(arrived))


def factor_kernel(chip_ref, own_keys, other_keys, drift_ref, part0, part1, part2, part3, sum_ref):
    chips = own_keys.shape[0]
    total = jnp.zeros(sum_ref.shape, jnp.float32)
    for turn, part_ref in enumerate((part0, part1, part2, part3)):
        source = lax.rem(chip_ref[0] + (chips - turn), chips)
        for side, keys_ref in enumerate((own_keys, other_keys)):
            total = total + lax.dot_general(
                keys_ref[source],
                part_ref[side],
                (((0,), (0,)), ((), ())),
                preferred_element_type=jnp.float32,
            )
    sum_ref[...] = drift_ref[...] + inner_rate * total


def factor_columns(chip, own_keys, other_keys, drift_factor, parts):
    return pl.pallas_call(
        factor_kernel,
        out_shape=jax.ShapeDtypeStruct(drift_factor.shape, jnp.float32),
        in_specs=[pl.BlockSpec(memory_space=pltpu.SMEM)] + [whole_vmem()] * 7,
        out_specs=whole_vmem(),
        compiler_params=kernel_params(),
        name="factor_columns",
    )(chip.reshape(1), own_keys, other_keys, drift_factor, *parts)


def branch_kernel(hidden_ref, back_ref, gain_ref, pieces_ref, out, out_sem):
    tokens, width = hidden_ref.shape
    chips, _, span = back_ref.shape
    rows = 16
    count = pieces_ref.shape[1]
    each = rows // count

    def departure(place):
        run = pl.ds(place * each, each)
        return pltpu.make_async_copy(out.at[run], pieces_ref.at[run], out_sem)

    def group(place, carry):
        lines = pl.ds(pl.multiple_of(place * rows, rows), rows)
        squares = jnp.zeros((rows, 128), jnp.float32)
        cross = jnp.zeros((rows, 128), jnp.float32)
        for chip in range(chips):
            for column in range(0, span, 128):
                at = chip * span + column
                value = hidden_ref[lines, at : at + 128].astype(jnp.float32)
                back = back_ref[chip, lines, column : column + 128].astype(jnp.float32)
                squares = squares + value * value
                cross = cross + value * (back * gain_ref[:, at : at + 128])
        recip = lax.rsqrt(jnp.sum(squares, -1, keepdims=True) / width + 1e-05)
        mean = jnp.sum(cross, -1, keepdims=True) * recip / width
        share = recip * recip * mean
        for chip in range(chips):
            for column in range(0, span, 128):
                at = chip * span + column
                value = hidden_ref[lines, at : at + 128].astype(jnp.float32)
                back = back_ref[chip, lines, column : column + 128].astype(jnp.float32)
                branch = recip * (back * gain_ref[:, at : at + 128]) - share * value
                branch = branch.astype(out.dtype)
                for part in range(each):
                    lines_of = branch[part * count : (part + 1) * count]
                    out[place * each + part, :, at : at + 128] = lines_of
        departure(place).start()
        return carry

    lax.fori_loop(0, tokens // rows, group, 0)
    pltpu.make_async_copy(out, pieces_ref, out_sem).wait()


def branch_pieces(hidden, back, gain_row, sections):
    tokens, width = hidden.shape
    shape = (sections, tokens // sections, width)
    return pl.pallas_call(
        branch_kernel,
        out_shape=pltpu.HBM(shape, jnp.bfloat16),
        in_specs=[whole_vmem()] * 3,
        out_specs=whole_hbm(),
        scratch_shapes=[pltpu.VMEM(shape, jnp.bfloat16), pltpu.SemaphoreType.DMA],
        compiler_params=kernel_params(),
        name="branch_pieces",
    )(pltpu.with_memory_space_constraint(hidden, pltpu.VMEM), back, gain_row)


def shards(hidden, norm_gain, key_grad, local_weight, drift, momentum, seeds):
    tokens, width = hidden.shape[2:]
    sections = lax.axis_size("section")
    islands = lax.axis_size("island")
    lanes = lax.axis_size("fsdp")
    chips = lanes // CORES
    lane = lax.axis_index("fsdp")
    chip, core = lane // CORES, lane - lane // CORES * CORES
    swap = [(i, i ^ 1) for i in range(lanes)]
    x_lines = [[c + CORES * i for i in range(chips)] for c in range(CORES)]
    gain_row = norm_gain
    own_hidden = hidden[0, 0]
    own_weight = local_weight[0, 0]
    slice_width = own_weight.shape[0]
    span = CORES * slice_width

    own_normed, swapped = prepare(core, own_hidden, gain_row, own_weight)
    swapped, sent_keys = lax.optimization_barrier((swapped, key_grad[0, 0]))
    arrived = lax.ppermute(swapped, "fsdp", swap)
    line_keys = lax.all_gather(sent_keys, "fsdp", axis_index_groups=x_lines)
    back = key_back_columns(core, line_keys, own_weight, arrived)
    back, own_normed, arrived = lax.optimization_barrier((back, own_normed, arrived))
    back = lax.all_to_all(back, "fsdp", 0, 0, axis_index_groups=x_lines)
    parts = list(pair_columns(chip, own_normed, arrived))
    for turn in (2, 1, 3):
        path = [(i, (i + CORES * turn) % lanes) for i in range(lanes)]
        parts[turn] = lax.ppermute(parts[turn], "fsdp", path)
    pieces = branch_pieces(own_hidden, back, gain_row, sections)
    pieces, *parts = lax.optimization_barrier((pieces, *parts))

    pieces = lax.all_to_all(pieces, "section", 0, 0)

    basis_row = projection_basis(seeds[0], line_keys.shape[2], RANK)
    own_keys = lax.dot_general(
        line_keys,
        basis_row.astype(jnp.bfloat16),
        (((2,), (0,)), ((), ())),
        preferred_element_type=jnp.float32,
    ).astype(jnp.bfloat16)
    other_keys = lax.ppermute(own_keys, "fsdp", swap)
    drift_factor = jnp.einsum("kr,dk->rd", basis_row, drift[0, 0], precision=lax.Precision.HIGH)
    factor = factor_columns(chip, own_keys, other_keys, drift_factor, parts)
    rank_share = momentum.shape[1]
    island = lax.axis_index("island")

    def rows_of(flip):
        at = jnp.bitwise_xor(island, flip) * rank_share
        return lax.dynamic_slice_in_dim(factor, at, rank_share, 0)

    def exchange(rows, flip):
        path = [(i, i ^ flip) for i in range(islands)]
        return lax.ppermute(rows.astype(jnp.bfloat16), "island", path).astype(jnp.float32)

    rows = exchange(jnp.concatenate([rows_of(1), rows_of(2)]), 1)
    own_sum = rows_of(0) + rows[:rank_share]
    other_sum = rows_of(3) + rows[rank_share:]
    pieces, own_sum, other_sum = lax.optimization_barrier((pieces, own_sum, other_sum))
    pieces = lax.all_to_all(suffix_sums(pieces), "section", 0, 0)
    input_grad = pieces.reshape(tokens, width)

    own_mean = (own_sum + exchange(other_sum, 3)) / islands
    own_momentum = momentum_rate * momentum[0] + own_mean
    own_step = (own_mean + momentum_rate * own_momentum).astype(jnp.bfloat16)
    step_factor = lax.all_gather(own_step, "island", axis=0, tiled=True).astype(jnp.float32)
    outer_update = outer_rate * jnp.einsum(
        "rd,kr->dk", step_factor, basis_row, precision=lax.Precision.HIGH
    )
    return (input_grad[None, None], own_momentum[None], outer_update[None])


def solution(mesh):
    return jax.shard_map(
        shards,
        mesh=mesh,
        in_specs=(
            P("island", "section", "fsdp", None),
            P("section", None),
            P("island", "section", "fsdp", None),
            P("island", "section", "fsdp", None),
            P("island", "section", "fsdp", None),
            P("section", "island", "fsdp"),
            P("section"),
        ),
        out_specs=(
            P("island", "section", "fsdp", None),
            P("section", "island", "fsdp"),
            P("section", "fsdp", None),
        ),
        check_vma=False,
    )
```

time: 177 us -> 133 us (0.75)
  the two profiles are of different devices: /device:TPU:2 before, /device:TPU:74 now
where the time goes in v2:
time: 133 us; the launch traced here: 132 us
  starting transfers between devices  51.5 us (39%)
  blocking collectives  35.2 us (26%)
  waiting for transfers between devices  23.3 us (18%)
  Pallas kernels  13 us (10%)
  matrix products  3.76 us (3%)
  local copies, waits for them, and re-layouts  2.82 us (2%)
  between operations  1.57 us (1%)
    all_gather x1, blocking collectives, shards(): lax.all_gather(own_step, 'island', axis=0, tiled=True).astype(jnp.float32)  21.7 us
    ppermute x2, starting transfers between devices, exchange(): lax.ppermute(rows.astype(jnp.bfloat16), 'island', path).astype(jnp.float32)  16.2 us
    all_gather x1, blocking collectives, shards(): line_keys = lax.all_gather(sent_keys, 'fsdp', axis_index_groups=x_lines)  13.5 us
    ppermute x3, starting transfers between devices, shards(): parts[turn] = lax.ppermute(parts[turn], 'fsdp', path)  10.4 us
    all_to_all x1, starting transfers between devices, shards(): pieces = lax.all_to_all(pieces, 'section', 0, 0)  8.6 us
    ppermute x2, waiting for transfers between devices, exchange(): lax.ppermute(rows.astype(jnp.bfloat16), 'island', path).astype(jnp.float32)  8.47 us
    all_to_all x1, starting transfers between devices, shards(): pieces = lax.all_to_all(suffix_sums(pieces), 'section', 0, 0)  7.8 us
    all_to_all x1, waiting for transfers between devices, shards(): pieces = lax.all_to_all(pieces, 'section', 0, 0)  6.59 us
  transfers between devices with their start and end apart: 10, of which 8 were waited for; matrix products, arithmetic and copies ran while one was open for 3% of the time, Pallas kernels for 5%

profile of v2, /device:TPU:74, one launch (start us, length us, event | category | flops | bytes accessed | tf_op | source)
XLA Modules:
  0.0 131.9 jit_solution(2463739648027048815)
XLA Ops:
  1.5 3.3 %prepare.1 = (bf16[4,128,512]{2,1,0:T(8,128)(2,1)}, bf16[1024,512]{1,0:T(8,128)(2,1)}) custom-call(s32[1]{0:T(128)} %bitcast.1.core_ref, bf16[128,4096]{1,0:T(8,128)(2,1)} %bitcast.26, f32[1,4096]{1,0:T(1,128)S(1)} %copy-done.6, bf16[512,512]{1,0:T(8,128)(2,1)} %bitcast.30), custom_call_target="tpu_custom_call" | custom-call | tf_op jit(solution)/shard_map/prepare/pallas_call | solution.py:216
  4.8 2.1 %collective-permute-start = (bf16[1024,512]{1,0:T(8,128)(2,1)}, bf16[1024,512]{1,0:T(8,128)(2,1)S(1)}, u32[]{:S(2)}, u32[]{:S(2)}) collective-permute-start(bf16[1024,512]{1,0:T(8,128)(2,1)} %get-tuple-element.24), channel_id=1, source_target_pairs={{0,1},{1,0},{2,3},{3,2},{4,5},{5,4},{6,7},{7,6},{8,9},{9,8},{10,11... | collective-permute-start | bytes 3145736 | tf_op jit(solution)/shard_map/ppermute | solution.py:384
  6.9 13.5 %all-gather = bf16[512,512]{1,0:T(8,128)(2,1)S(1)} all-gather(bf16[128,512]{1,0:T(8,128)(2,1)S(1)} %bitcast.33), channel_id=2, replica_groups={{0,2,4,6},{1,3,5,7},{8,10,12,14},{9,11,13,15},{16,18,20,22},{17,19,21,2..., dimensions={0}, use_global_device_ids=true | all-gather | bytes 655360 | tf_op jit(solution)/shard_map/all_gather | solution.py:385
  21.4 2.6 %key_back_columns.1 = bf16[4,128,1024]{2,1,0:T(8,128)(2,1)} custom-call(s32[1]{0:T(128)} %bitcast.1.core_ref, bf16[4,128,512]{2,1,0:T(8,128)(2,1)S(1)} %bitcast.28, bf16[512,512]{1,0:T(8,128)(2,1)S(1)} %bitcast.31, bf16[1024,512]{1,0:T(8,128)(2,1)} %copy-done.7), custom_call_target="tpu_custom_call" | custom-call | tf_op jit(solution)/shard_map/key_back_columns/pallas_call | solution.py:116
  24.0 4.5 %all-to-all-start = ((bf16[4,128,1024]{2,1,0:T(8,128)(2,1)}), bf16[4,128,1024]{2,1,0:T(8,128)(2,1)S(1)}, u32[]{:S(2)}, u32[]{:S(2)}) async-start(bf16[4,128,1024]{2,1,0:T(8,128)(2,1)} %key_back_columns.1), calls=%async_computation | async-start | bytes 2097152 | tf_op jit(solution)/shard_map/all_to_all | solution.py:388
  28.5 2.2 %pair_columns.1 = (bf16[2,128,512]{2,1,0:T(8,128)(2,1)}, bf16[2,128,512]{2,1,0:T(8,128)(2,1)}, bf16[2,128,512]{2,1,0:T(8,128)(2,1)}, bf16[2,128,512]{2,1,0:T(8,128)(2,1)}) custom-call(s32[1]{0:T(128)} %bitcast.5.chip_ref, bf16[4,128,512]{2,1,0:T(8,128)(2,1)} %get-tuple-element.27.own_ref, bf16[1024,512]{1,0:T(8,128)(2,1)} %copy-done.7), custom_call_target="tpu_custom_call" | custom-call | tf_op jit(solution)/shard_map/pair_columns/pallas_call | solution.py:269
  30.7 3.4 %collective-permute-start.1 = (bf16[2,128,512]{2,1,0:T(8,128)(2,1)}, bf16[2,128,512]{2,1,0:T(8,128)(2,1)S(1)}, u32[]{:S(2)}, u32[]{:S(2)}) collective-permute-start(bf16[2,128,512]{2,1,0:T(8,128)(2,1)} %get-tuple-element.30), channel_id=1, source_target_pairs={{0,2},{1,3},{2,4},{3,5},{4,6},{5,7},{6,0},{7,1},{8,10},{9,11},{10,... | collective-permute-start | bytes 786440 | tf_op jit(solution)/shard_map/ppermute | solution.py:392
  34.1 2.5 %collective-permute-start.2 = (bf16[2,128,512]{2,1,0:T(8,128)(2,1)}, bf16[2,128,512]{2,1,0:T(8,128)(2,1)}, u32[]{:S(2)}, u32[]{:S(2)}) collective-permute-start(bf16[2,128,512]{2,1,0:T(8,128)(2,1)} %get-tuple-element.31), channel_id=1, source_target_pairs={{0,4},{1,5},{2,6},{3,7},{4,0},{5,1},{6,2},{7,3},{8,12},{9,13},{10,... | collective-permute-start | bytes 786440 | tf_op jit(solution)/shard_map/ppermute | solution.py:392
  36.6 4.5 %collective-permute-start.3 = (bf16[2,128,512]{2,1,0:T(8,128)(2,1)}, bf16[2,128,512]{2,1,0:T(8,128)(2,1)}, u32[]{:S(2)}, u32[]{:S(2)}) collective-permute-start(bf16[2,128,512]{2,1,0:T(8,128)(2,1)} %get-tuple-element.32), channel_id=1, source_target_pairs={{0,6},{1,7},{2,0},{3,1},{4,2},{5,3},{6,4},{7,5},{8,14},{9,15},{10,... | collective-permute-start | bytes 786440 | tf_op jit(solution)/shard_map/ppermute | solution.py:392
  41.2 1.7 %all-to-all-done.back_ref = bf16[4,128,1024]{2,1,0:T(8,128)(2,1)S(1)} async-done(((bf16[4,128,1024]{2,1,0:T(8,128)(2,1)}), bf16[4,128,1024]{2,1,0:T(8,128)(2,1)S(1)}, u32[]{:S(2)}, u32[]{:S(2)}) %all-to-all-start) | async-done | bytes 1048608 | tf_op jit(solution)/shard_map/all_to_all | solution.py:388
  42.9 2.1 %branch_pieces.1 = bf16[16,8,4096]{2,1,0:T(8,128)(2,1)} custom-call(bf16[128,4096]{1,0:T(8,128)(2,1)S(1)} %bitcast.27, bf16[4,128,1024]{2,1,0:T(8,128)(2,1)S(1)} %all-to-all-done.back_ref, f32[1,4096]{1,0:T(1,128)S(1)} %copy-done.6), custom_call_target="tpu_custom_call" | custom-call | tf_op jit(solution)/shard_map/branch_pieces/pallas_call | solution.py:355
  46.7 1.9 %collective-permute-done.2.part2 = bf16[2,128,512]{2,1,0:T(8,128)(2,1)} collective-permute-done((bf16[2,128,512]{2,1,0:T(8,128)(2,1)}, bf16[2,128,512]{2,1,0:T(8,128)(2,1)}, u32[]{:S(2)}, u32[]{:S(2)}) %collective-permute-start.2) | collective-permute-done | bytes 262176 | tf_op jit(solution)/shard_map/ppermute | solution.py:392
  48.6 2.8 %collective-permute-done.3.part3 = bf16[2,128,512]{2,1,0:T(8,128)(2,1)} collective-permute-done((bf16[2,128,512]{2,1,0:T(8,128)(2,1)}, bf16[2,128,512]{2,1,0:T(8,128)(2,1)}, u32[]{:S(2)}, u32[]{:S(2)}) %collective-permute-start.3) | collective-permute-done | bytes 262176 | tf_op jit(solution)/shard_map/ppermute | solution.py:392
  51.3 8.6 %all-to-all-start.1 = ((bf16[16,8,4096]{2,1,0:T(8,128)(2,1)}), bf16[16,8,4096]{2,1,0:T(8,128)(2,1)S(1)}, u32[]{:S(2)}, u32[]{:S(2)}) async-start(bf16[16,8,4096]{2,1,0:T(8,128)(2,1)} %branch_pieces.1), calls=%async_computation.1 | async-start | bytes 2097152 | tf_op jit(solution)/shard_map/all_to_all | solution.py:396
  61.2 1.9 %collective-permute-start.4 = (bf16[4,128,256]{2,1,0:T(8,128)(2,1)S(1)}, bf16[4,128,256]{2,1,0:T(8,128)(2,1)S(1)}, u32[]{:S(2)}, u32[]{:S(2)}) collective-permute-start(bf16[4,128,256]{2,1,0:T(8,128)(2,1)S(1)} %convolution_convert_fusion.own_keys), channel_id=1, source_target_pairs={{0,1},{1,0},{2,3},{3,2},{4,5},{5,4},{6,7},{7,6},{8,9},{9,8},{10,11... | collective-permute-start | bytes 786440 | tf_op jit(solution)/shard_map/ppermute | solution.py:405
  64.7 1.8 %factor_columns.1 = f32[256,512]{1,0:T(8,128)S(1)} custom-call(s32[1]{0:T(128)} %bitcast.5.chip_ref, bf16[4,128,256]{2,1,0:T(8,128)(2,1)S(1)} %convolution_convert_fusion.own_keys, bf16[4,128,256]{2,1,0:T(8,128)(2,1)S(1)} %collective-permute-done.4.other_keys, f32[256,512]{1,0:T(8,128)S(1)} %fusion.1.drift_ref, bf16[2,128,512]{2,1,0:T(8,128)(2,1)S(1)} %copy-done.5, ...), custom_call_target="tpu_custom_call" | custom-call | tf_op jit(solution)/shard_map/factor_columns/pallas_call | solution.py:300
  66.5 6.1 %collective-permute-start.5 = (bf16[128,512]{1,0:T(8,128)(2,1)S(1)}, bf16[128,512]{1,0:T(8,128)(2,1)S(1)}, u32[]{:S(2)}, u32[]{:S(2)}) collective-permute-start(bf16[128,512]{1,0:T(8,128)(2,1)S(1)} %pad_maximum_fusion), channel_id=1, source_target_pairs={{0,128},{128,0},{256,384},{384,256},{1,129},{129,1},{257,385},{385... | collective-permute-start | bytes 393224 | tf_op jit(solution)/shard_map/ppermute | solution.py:417
  72.6 5.4 %collective-permute-done.5 = bf16[128,512]{1,0:T(8,128)(2,1)S(1)} collective-permute-done((bf16[128,512]{1,0:T(8,128)(2,1)S(1)}, bf16[128,512]{1,0:T(8,128)(2,1)S(1)}, u32[]{:S(2)}, u32[]{:S(2)}) %collective-permute-start.5) | collective-permute-done | bytes 131104 | tf_op jit(solution)/shard_map/ppermute | solution.py:417
  78.1 6.6 %all-to-all-done.1.parts_ref = bf16[16,8,4096]{2,1,0:T(8,128)(2,1)S(1)} async-done(((bf16[16,8,4096]{2,1,0:T(8,128)(2,1)}), bf16[16,8,4096]{2,1,0:T(8,128)(2,1)S(1)}, u32[]{:S(2)}, u32[]{:S(2)}) %all-to-all-start.1) | async-done | bytes 1048608 | tf_op jit(solution)/shard_map/all_to_all | solution.py:396
  85.7 7.8 %all-to-all-start.2 = ((bf16[16,8,4096]{2,1,0:T(8,128)(2,1)}), bf16[16,8,4096]{2,1,0:T(8,128)(2,1)S(1)}, u32[]{:S(2)}, u32[]{:S(2)}) async-start(bf16[16,8,4096]{2,1,0:T(8,128)(2,1)} %suffix_sums.1), calls=%async_computation.2 | async-start | bytes 2097152 | tf_op jit(solution)/shard_map/all_to_all | solution.py:423
  93.5 10.1 %collective-permute-start.6 = (bf16[64,512]{1,0:T(8,128)(2,1)S(1)}, bf16[64,512]{1,0:T(8,128)(2,1)S(1)}, u32[]{:S(2)}, u32[]{:S(2)}) collective-permute-start(bf16[64,512]{1,0:T(8,128)(2,1)S(1)} %slice_add_fusion), channel_id=1, source_target_pairs={{0,384},{128,256},{256,128},{384,0},{1,385},{129,257},{257,129},{3... | collective-permute-start | bytes 196616 | tf_op jit(solution)/shard_map/ppermute | solution.py:417
  103.6 3.1 %collective-permute-done.6 = bf16[64,512]{1,0:T(8,128)(2,1)S(1)} collective-permute-done((bf16[64,512]{1,0:T(8,128)(2,1)S(1)}, bf16[64,512]{1,0:T(8,128)(2,1)S(1)}, u32[]{:S(2)}, u32[]{:S(2)}) %collective-permute-start.6) | collective-permute-done | bytes 65568 | tf_op jit(solution)/shard_map/ppermute | solution.py:417
  107.4 21.7 %all_gather.11 = bf16[256,512]{1,0:T(8,128)(2,1)S(1)} all-gather(bf16[64,512]{1,0:T(8,128)(2,1)S(1)} %get-tuple-element.43), channel_id=1, replica_groups=mesh['island'=4,'section'=16,'fsdp'=8] {'island'}, dimensions={0}, use_global_device_ids=true | all-gather | bytes 327680 | tf_op jit(solution)/shard_map/all_gather | solution.py:429
  129.1 1.8 %fusion = f32[1,512,512]{2,1,0:T(8,128)} fusion(bf16[256,512]{1,0:T(8,128)(2,1)S(1)} %all_gather.11, s32[]{:T(128)} %bitcast.6, s32[512]{0:T(512)S(1)} %iota_multiply_fusion), kind=kOutput, calls=%fused_computation.1 | convolution fusion | flops 405012480 | bytes 1312772 | tf_op jit(solution)/shard_map/rd,kr->dk/dot_general | solution.py:430
  (35 shorter events, 8.4 us)
Async XLA Ops:
  0.6 62.6 %copy-start = (f32[1,1,512,512]{3,2,1,0:T(8,128)S(1)}, f32[1,1,512,512]{3,2,1,0:T(8,128)}, u32[]{:S(2)}) copy-start(f32[1,1,512,512]{3,2,1,0:T(8,128)} %param.11) | copy-start | bytes 3145732
  0.7 0.8 copy-start.6
  1.5 5.4 %copy-start.8 = (bf16[1,1,128,512]{3,2,1,0:T(8,128)(2,1)S(1)}, bf16[1,1,128,512]{3,2,1,0:T(8,128)(2,1)}, u32[]{:S(2)}) copy-start(bf16[1,1,128,512]{3,2,1,0:T(8,128)(2,1)} %param.9) | copy-start | bytes 393220
  4.8 16.6 %copy-start.4 = (bf16[1,1,512,512]{3,2,1,0:T(8,128)(2,1)S(1)}, bf16[1,1,512,512]{3,2,1,0:T(8,128)(2,1)}, u32[]{:S(2)}) copy-start(bf16[1,1,512,512]{3,2,1,0:T(8,128)(2,1)} %param.10) | copy-start | bytes 1572868
  4.8 15.6 %collective-permute-start = (bf16[1024,512]{1,0:T(8,128)(2,1)}, bf16[1024,512]{1,0:T(8,128)(2,1)S(1)}, u32[]{:S(2)}, u32[]{:S(2)}) collective-permute-start(bf16[1024,512]{1,0:T(8,128)(2,1)} %get-tuple-element.24), channel_id=1, source_target_pairs={{0,1},{1,0},{2,3},{3,2},{4,5},{5,4},{6,7},{7,6},{8,9},{9,8},{10,11... | collective-permute-start | bytes 3145736 | tf_op jit(solution)/shard_map/ppermute | solution.py:384
  20.4 3.6 %copy-start.2 = (bf16[512,512]{1,0:T(8,128)(2,1)}, bf16[512,512]{1,0:T(8,128)(2,1)S(1)}, u32[]{:S(2)}) copy-start(bf16[512,512]{1,0:T(8,128)(2,1)S(1)} %all-gather) | copy-start | bytes 1572868
  20.4 1.0 copy-start.7
  24.0 18.9 %all-to-all-start = ((bf16[4,128,1024]{2,1,0:T(8,128)(2,1)}), bf16[4,128,1024]{2,1,0:T(8,128)(2,1)S(1)}, u32[]{:S(2)}, u32[]{:S(2)}) async-start(bf16[4,128,1024]{2,1,0:T(8,128)(2,1)} %key_back_columns.1), calls=%async_computation | async-start | bytes 2097152 | tf_op jit(solution)/shard_map/all_to_all | solution.py:388
  28.5 14.4 %copy-start.1 = (bf16[1,1,128,4096]{3,2,1,0:T(8,128)(2,1)S(1)}, bf16[1,1,128,4096]{3,2,1,0:T(8,128)(2,1)}, u32[]{:S(2)}) copy-start(bf16[1,1,128,4096]{3,2,1,0:T(8,128)(2,1)} %param.7) | copy-start | bytes 3145732
  30.7 16.0 %collective-permute-start.1 = (bf16[2,128,512]{2,1,0:T(8,128)(2,1)}, bf16[2,128,512]{2,1,0:T(8,128)(2,1)S(1)}, u32[]{:S(2)}, u32[]{:S(2)}) collective-permute-start(bf16[2,128,512]{2,1,0:T(8,128)(2,1)} %get-tuple-element.30), channel_id=1, source_target_pairs={{0,2},{1,3},{2,4},{3,5},{4,6},{5,7},{6,0},{7,1},{8,10},{9,11},{10,... | collective-permute-start | bytes 786440 | tf_op jit(solution)/shard_map/ppermute | solution.py:392
  34.1 14.5 %collective-permute-start.2 = (bf16[2,128,512]{2,1,0:T(8,128)(2,1)}, bf16[2,128,512]{2,1,0:T(8,128)(2,1)}, u32[]{:S(2)}, u32[]{:S(2)}) collective-permute-start(bf16[2,128,512]{2,1,0:T(8,128)(2,1)} %get-tuple-element.31), channel_id=1, source_target_pairs={{0,4},{1,5},{2,6},{3,7},{4,0},{5,1},{6,2},{7,3},{8,12},{9,13},{10,... | collective-permute-start | bytes 786440 | tf_op jit(solution)/shard_map/ppermute | solution.py:392
  36.6 14.7 %collective-permute-start.3 = (bf16[2,128,512]{2,1,0:T(8,128)(2,1)}, bf16[2,128,512]{2,1,0:T(8,128)(2,1)}, u32[]{:S(2)}, u32[]{:S(2)}) collective-permute-start(bf16[2,128,512]{2,1,0:T(8,128)(2,1)} %get-tuple-element.32), channel_id=1, source_target_pairs={{0,6},{1,7},{2,0},{3,1},{4,2},{5,3},{6,4},{7,5},{8,14},{9,15},{10,... | collective-permute-start | bytes 786440 | tf_op jit(solution)/shard_map/ppermute | solution.py:392
  51.3 9.3 %copy-start.3 = (bf16[512,512]{1,0:T(8,128)(2,1)S(1)}, bf16[512,512]{1,0:T(8,128)(2,1)}, u32[]{:S(2)}) copy-start(bf16[512,512]{1,0:T(8,128)(2,1)} %copy-done.2) | copy-start | bytes 1572868
  51.3 33.3 %all-to-all-start.1 = ((bf16[16,8,4096]{2,1,0:T(8,128)(2,1)}), bf16[16,8,4096]{2,1,0:T(8,128)(2,1)S(1)}, u32[]{:S(2)}, u32[]{:S(2)}) async-start(bf16[16,8,4096]{2,1,0:T(8,128)(2,1)} %branch_pieces.1), calls=%async_computation.1 | async-start | bytes 2097152 | tf_op jit(solution)/shard_map/all_to_all | solution.py:396
  61.2 3.4 %collective-permute-start.4 = (bf16[4,128,256]{2,1,0:T(8,128)(2,1)S(1)}, bf16[4,128,256]{2,1,0:T(8,128)(2,1)S(1)}, u32[]{:S(2)}, u32[]{:S(2)}) collective-permute-start(bf16[4,128,256]{2,1,0:T(8,128)(2,1)S(1)} %convolution_convert_fusion.own_keys), channel_id=1, source_target_pairs={{0,1},{1,0},{2,3},{3,2},{4,5},{5,4},{6,7},{7,6},{8,9},{9,8},{10,11... | collective-permute-start | bytes 786440 | tf_op jit(solution)/shard_map/ppermute | solution.py:405
  63.2 1.5 %copy-start.5 = (bf16[2,128,512]{2,1,0:T(8,128)(2,1)S(1)}, bf16[2,128,512]{2,1,0:T(8,128)(2,1)}, u32[]{:S(2)}) copy-start(bf16[2,128,512]{2,1,0:T(8,128)(2,1)} %get-tuple-element.34.part0) | copy-start | bytes 786436
  66.5 11.5 %collective-permute-start.5 = (bf16[128,512]{1,0:T(8,128)(2,1)S(1)}, bf16[128,512]{1,0:T(8,128)(2,1)S(1)}, u32[]{:S(2)}, u32[]{:S(2)}) collective-permute-start(bf16[128,512]{1,0:T(8,128)(2,1)S(1)} %pad_maximum_fusion), channel_id=1, source_target_pairs={{0,128},{128,0},{256,384},{384,256},{1,129},{129,1},{257,385},{385... | collective-permute-start | bytes 393224 | tf_op jit(solution)/shard_map/ppermute | solution.py:417
  85.7 21.0 %copy-start.9 = (f32[1,64,512]{2,1,0:T(8,128)S(1)}, f32[1,64,512]{2,1,0:T(8,128)}, u32[]{:S(2)}) copy-start(f32[1,64,512]{2,1,0:T(8,128)} %param.12) | copy-start | bytes 393220
  85.7 45.2 %all-to-all-start.2 = ((bf16[16,8,4096]{2,1,0:T(8,128)(2,1)}), bf16[16,8,4096]{2,1,0:T(8,128)(2,1)S(1)}, u32[]{:S(2)}, u32[]{:S(2)}) async-start(bf16[16,8,4096]{2,1,0:T(8,128)(2,1)} %suffix_sums.1), calls=%async_computation.2 | async-start | bytes 2097152 | tf_op jit(solution)/shard_map/all_to_all | solution.py:423
  93.5 13.2 %collective-permute-start.6 = (bf16[64,512]{1,0:T(8,128)(2,1)S(1)}, bf16[64,512]{1,0:T(8,128)(2,1)S(1)}, u32[]{:S(2)}, u32[]{:S(2)}) collective-permute-start(bf16[64,512]{1,0:T(8,128)(2,1)S(1)} %slice_add_fusion), channel_id=1, source_target_pairs={{0,384},{128,256},{256,128},{384,0},{1,385},{129,257},{257,129},{3... | collective-permute-start | bytes 196616 | tf_op jit(solution)/shard_map/ppermute | solution.py:417

commit v3 on v2

--- a/solution.py
+++ b/solution.py
@@ -36,12 +36,20 @@
     return pl.BlockSpec(memory_space=pltpu.HBM)
 
 
+def anywhere():
+    return pl.BlockSpec(memory_space=pl.ANY)
+
+
+def in_vmem(array):
+    return pltpu.with_memory_space_constraint(array, pltpu.VMEM)
+
+
 def in_hbm(array):
     return pltpu.with_memory_space_constraint(array, pltpu.HBM)
 
 
 def kernel_params():
-    return pltpu.CompilerParams(vmem_limit_bytes=24 * 1024 * 1024)
+    return pltpu.CompilerParams(vmem_limit_bytes=8 * 1024 * 1024)
 
 
 def suffix_kernel(parts_ref, sums_ref, out, out_sems):
@@ -81,52 +89,48 @@
     )(pltpu.with_memory_space_constraint(parts, pltpu.VMEM))
 
 
-def key_back_kernel(
-    core_ref, keys_ref, own_ref, other_ref, back_ref, held, out, held_sem, out_sems
-):
-    chips = keys_ref.shape[0]
+def key_back_kernel(core_ref, keys_ref, own_ref, other_ref, back_ref, out, out_sems):
+    chips, tokens, depth = keys_ref.shape
     width = own_ref.shape[0]
     core = core_ref[0]
-    arrival = pltpu.make_async_copy(other_ref.at[pl.ds(0, width)], held, held_sem)
-    arrival.start()
-
-    def departure(chip):
-        return pltpu.make_async_copy(out.at[chip], back_ref.at[chip], out_sems.at[chip])
-
-    for weight_ref, place in ((own_ref, core), (held, 1 - core)):
-        span = pl.ds(pl.multiple_of(place * width, width), width)
-        if weight_ref is held:
-            arrival.wait()
-        for chip in range(chips):
-            out[chip, :, span] = lax.dot_general(
-                keys_ref[chip],
-                weight_ref[...],
-                (((1,), (1,)), ((), ())),
-                preferred_element_type=jnp.float32,
-            ).astype(out.dtype)
-            if weight_ref is held:
-                departure(chip).start()
-    for chip in range(chips):
-        departure(chip).wait()
+    keys = keys_ref[...].reshape(chips * tokens, depth)
+
+    def departure(side, chip):
+        span = pl.ds(pl.multiple_of((core if side == 0 else 1 - core) * width, width), width)
+        return pltpu.make_async_copy(
+            out.at[side, chip], back_ref.at[chip, :, span], out_sems.at[side, chip]
+        )
+
+    for side, weight_ref in enumerate((own_ref, other_ref)):
+        product = lax.dot_general(
+            keys,
+            weight_ref[0:width, :],
+            (((1,), (1,)), ((), ())),
+            preferred_element_type=jnp.float32,
+        ).astype(out.dtype)
+        for chip in range(chips):
+            out[side, chip] = product[chip * tokens : (chip + 1) * tokens]
+            departure(side, chip).start()
+    for side in range(CORES):
+        for chip in range(chips):
+            departure(side, chip).wait()
 
 
 def key_back_columns(core, keys, own_weight, arrived):
     chips, tokens, _ = keys.shape
-    shape = (chips, tokens, CORES * own_weight.shape[0])
+    width = own_weight.shape[0]
     return pl.pallas_call(
         key_back_kernel,
-        out_shape=pltpu.HBM(shape, jnp.bfloat16),
-        in_specs=[pl.BlockSpec(memory_space=pltpu.SMEM), whole_vmem(), whole_vmem(), whole_hbm()],
+        out_shape=pltpu.HBM((chips, tokens, CORES * width), jnp.bfloat16),
+        in_specs=[pl.BlockSpec(memory_space=pltpu.SMEM)] + [whole_vmem()] * 3,
         out_specs=whole_hbm(),
         scratch_shapes=[
-            pltpu.VMEM(own_weight.shape, own_weight.dtype),
-            pltpu.VMEM(shape, jnp.bfloat16),
-            pltpu.SemaphoreType.DMA,
-            pltpu.SemaphoreType.DMA((chips,)),
+            pltpu.VMEM((CORES, chips, tokens, width), jnp.bfloat16),
+            pltpu.SemaphoreType.DMA((CORES, chips)),
         ],
         compiler_params=kernel_params(),
         name="key_back_columns",
-    )(core.reshape(1), keys, own_weight, in_hbm(arrived))
+    )(core.reshape(1), keys, own_weight, arrived)
 
 
 def prepare_kernel(
@@ -137,73 +141,67 @@
     own_ref,
     swap_ref,
     held,
-    own_out,
-    swap_out,
+    gain,
+    outs,
     weight,
     held_sems,
-    own_sems,
-    swap_sems,
+    out_sems,
 ):
     tokens, width = hidden_ref.shape
     chips, _, slice_width = own_ref.shape
-    chunks = held_sems.shape[0] - 1
+    chunks = out_sems.shape[1]
     core = core_ref[0]
-    rows = 16
-    each = tokens // chunks
+    rows = tokens // chunks
 
     def arrival(chunk):
-        lines = pl.ds(chunk * each, each)
+        lines = pl.ds(chunk * rows, rows)
         return pltpu.make_async_copy(hidden_ref.at[lines], held.at[lines], held_sems.at[chunk])
 
-    weight_in = pltpu.make_async_copy(weight_ref, weight, held_sems.at[chunks])
+    def departures(chunk):
+        lines = pl.ds(chunk * rows, rows)
+        for chip in range(chips):
+            below = pl.ds(slice_width + chip * tokens + chunk * rows, rows)
+            for side, place in enumerate((own_ref.at[chip, lines], swap_ref.at[below])):
+                yield pltpu.make_async_copy(
+                    outs.at[side, chip, lines], place, out_sems.at[side, chunk, chip]
+                )
+
+    gain_in = pltpu.make_async_copy(gain_ref, gain, held_sems.at[chunks])
+    weight_in = pltpu.make_async_copy(weight_ref, weight, held_sems.at[chunks + 1])
     weight_out = pltpu.make_async_copy(
-        weight, swap_ref.at[pl.ds(0, slice_width)], swap_sems.at[chips]
+        weight, swap_ref.at[pl.ds(0, slice_width)], held_sems.at[chunks + 2]
     )
-    for chunk in range(chunks):
+    arrival(0).start()
+    gain_in.start()
+    for chunk in range(1, chunks):
         arrival(chunk).start()
     weight_in.start()
-
-    def group(place, carry):
-        lines = pl.ds(pl.multiple_of(place * rows, rows), rows)
-        squares = jnp.zeros((rows, 128), jnp.float32)
-        for at in range(0, width, 128):
-            value = held[lines, at : at + 128].astype(jnp.float32)
-            squares = squares + value * value
-        recip = lax.rsqrt(jnp.sum(squares, -1, keepdims=True) / width + 1e-05)
-
-        def normed(chip, side):
-            at = pl.multiple_of((CORES * chip + side) * slice_width, slice_width)
-            span = pl.ds(at, slice_width)
-            value = held[lines, span].astype(jnp.float32) * recip
-            return (value * gain_ref[:, span]).astype(own_out.dtype)
-
-        for chip in range(chips):
-            own_out[chip, lines, :] = normed(chip, core)
-            swap_out[chip, lines, :] = normed(chip, 1 - core)
-        return carry
-
+    gain_in.wait()
     for chunk in range(chunks):
         arrival(chunk).wait()
-        lax.fori_loop(chunk * each // rows, (chunk + 1) * each // rows, group, 0)
+        lines = pl.ds(chunk * rows, rows)
+        squares = [jnp.zeros((rows, 128), jnp.float32)] * 2
+        for column in range(0, width // 128):
+            value = held[lines, column * 128 : column * 128 + 128].astype(jnp.float32)
+            squares[column % 2] = squares[column % 2] + value * value
+        total = jnp.sum(squares[0] + squares[1], -1, keepdims=True)
+        recip = lax.rsqrt(total / width + 1e-05)
+        for chip in range(chips):
+            for side, place in enumerate((core, 1 - core)):
+                first = pl.multiple_of((CORES * chip + place) * slice_width, slice_width)
+                for column in range(0, slice_width, 128):
+                    span = pl.ds(pl.multiple_of(first + column, 128), 128)
+                    value = held[lines, span].astype(jnp.float32) * recip
+                    normed = (value * gain[:, span]).astype(outs.dtype)
+                    outs[side, chip, lines, column : column + 128] = normed
+        for copy in departures(chunk):
+            copy.start()
         if chunk == 0:
             weight_in.wait()
             weight_out.start()
-
-    def departures(chip):
-        at = slice_width + chip * tokens
-        return (
-            pltpu.make_async_copy(
-                swap_out.at[chip], swap_ref.at[pl.ds(at, tokens)], swap_sems.at[chip]
-            ),
-            pltpu.make_async_copy(own_out.at[chip], own_ref.at[chip], own_sems.at[chip]),
-        )
-
-    for chip in range(chips):
-        for copy in departures(chip):
-            copy.start()
     weight_out.wait()
-    for chip in range(chips):
-        for copy in departures(chip):
+    for chunk in range(chunks):
+        for copy in departures(chunk):
             copy.wait()
 
 
@@ -219,25 +217,19 @@
             pltpu.HBM(columns, jnp.bfloat16),
             pltpu.HBM((slice_width + chips * tokens, key_width), jnp.bfloat16),
         ),
-        in_specs=[
-            pl.BlockSpec(memory_space=pltpu.SMEM),
-            whole_hbm(),
-            whole_vmem(),
-            whole_hbm(),
-        ],
+        in_specs=[pl.BlockSpec(memory_space=pltpu.SMEM)] + [whole_hbm()] * 3,
         out_specs=(whole_hbm(),) * 2,
         scratch_shapes=[
             pltpu.VMEM(hidden.shape, hidden.dtype),
-            pltpu.VMEM(columns, jnp.bfloat16),
-            pltpu.VMEM(columns, jnp.bfloat16),
+            pltpu.VMEM(gain_row.shape, gain_row.dtype),
+            pltpu.VMEM((CORES, *columns), jnp.bfloat16),
             pltpu.VMEM(weight.shape, weight.dtype),
-            pltpu.SemaphoreType.DMA((chunks + 1,)),
-            pltpu.SemaphoreType.DMA((chips,)),
-            pltpu.SemaphoreType.DMA((chips + 1,)),
+            pltpu.SemaphoreType.DMA((chunks + 3,)),
+            pltpu.SemaphoreType.DMA((CORES, chunks, chips)),
         ],
         compiler_params=kernel_params(),
         name="prepare",
-    )(core.reshape(1), in_hbm(hidden), gain_row, in_hbm(weight))
+    )(core.reshape(1), in_hbm(hidden), in_hbm(gain_row), in_hbm(weight))
 
 
 def pair_kernel(chip_ref, own_ref, other_ref, *refs):
@@ -269,7 +261,7 @@
     return pl.pallas_call(
         pair_kernel,
         out_shape=(pltpu.HBM(shape, own_normed.dtype),) * chips,
-        in_specs=[pl.BlockSpec(memory_space=pltpu.SMEM)] + [whole_hbm()] * 2,
+        in_specs=[pl.BlockSpec(memory_space=pltpu.SMEM), whole_hbm(), anywhere()],
         out_specs=(whole_hbm(),) * chips,
         scratch_shapes=[
             pltpu.VMEM((chips, *shape), own_normed.dtype),
@@ -278,7 +270,7 @@
         ],
         compiler_params=kernel_params(),
         name="pair_columns",
-    )(chip.reshape(1), in_hbm(own_normed), in_hbm(arrived))
+    )(chip.reshape(1), in_hbm(own_normed), arrived)
 
 
 def factor_kernel(chip_ref, own_keys, other_keys, drift_ref, part0, part1, part2, part3, sum_ref):
@@ -387,14 +379,6 @@
     back, own_normed, arrived = lax.optimization_barrier((back, own_normed, arrived))
     back = lax.all_to_all(back, "fsdp", 0, 0, axis_index_groups=x_lines)
     parts = list(pair_columns(chip, own_normed, arrived))
-    for turn in (2, 1, 3):
-        path = [(i, (i + CORES * turn) % lanes) for i in range(lanes)]
-        parts[turn] = lax.ppermute(parts[turn], "fsdp", path)
-    pieces = branch_pieces(own_hidden, back, gain_row, sections)
-    pieces, *parts = lax.optimization_barrier((pieces, *parts))
-
-    pieces = lax.all_to_all(pieces, "section", 0, 0)
-
     basis_row = projection_basis(seeds[0], line_keys.shape[2], RANK)
     own_keys = lax.dot_general(
         line_keys,
@@ -403,6 +387,16 @@
         preferred_element_type=jnp.float32,
     ).astype(jnp.bfloat16)
     other_keys = lax.ppermute(own_keys, "fsdp", swap)
+    back, own_keys, other_keys, *parts = lax.optimization_barrier(
+        (back, own_keys, other_keys, *parts)
+    )
+    pieces = branch_pieces(own_hidden, back, gain_row, sections)
+
+    pieces = lax.all_to_all(pieces, "section", 0, 0)
+
+    for turn in (2, 1, 3):
+        path = [(i, (i + CORES * turn) % lanes) for i in range(lanes)]
+        parts[turn] = lax.ppermute(parts[turn], "fsdp", path)
     drift_factor = jnp.einsum("kr,dk->rd", basis_row, drift[0, 0], precision=lax.Precision.HIGH)
     factor = factor_columns(chip, own_keys, other_keys, drift_factor, parts)
     rank_share = momentum.shape[1]
@@ -419,16 +413,21 @@
     rows = exchange(jnp.concatenate([rows_of(1), rows_of(2)]), 1)
     own_sum = rows_of(0) + rows[:rank_share]
     other_sum = rows_of(3) + rows[rank_share:]
-    pieces, own_sum, other_sum = lax.optimization_barrier((pieces, own_sum, other_sum))
-    pieces = lax.all_to_all(suffix_sums(pieces), "section", 0, 0)
+    sums, own_sum, other_sum = lax.optimization_barrier((suffix_sums(pieces), own_sum, other_sum))
+    pieces = lax.all_to_all(sums, "section", 0, 0)
     input_grad = pieces.reshape(tokens, width)
 
-    own_mean = (own_sum + exchange(other_sum, 3)) / islands
+    mean_weight = (1.0 + momentum_rate) / islands
+    ride = momentum_rate * momentum_rate / mean_weight
+    pair_sums = jnp.stack([own_sum + ride * momentum[0], other_sum]).astype(jnp.bfloat16)
+    pair_sums = lax.all_gather(pair_sums, "island")
+    other_pair = lax.dynamic_index_in_dim(pair_sums, jnp.bitwise_xor(island, 3), 0, False)[1]
+    own_mean = (own_sum + other_pair.astype(jnp.float32)) / islands
     own_momentum = momentum_rate * momentum[0] + own_mean
-    own_step = (own_mean + momentum_rate * own_momentum).astype(jnp.bfloat16)
-    step_factor = lax.all_gather(own_step, "island", axis=0, tiled=True).astype(jnp.float32)
-    outer_update = outer_rate * jnp.einsum(
-        "rd,kr->dk", step_factor, basis_row, precision=lax.Precision.HIGH
+    pair_sums = pair_sums.astype(jnp.float32)
+    total = jnp.concatenate([pair_sums[i, 0] + pair_sums[i ^ 3, 1] for i in range(islands)])
+    outer_update = (outer_rate * mean_weight) * jnp.einsum(
+        "rd,kr->dk", total, basis_row, precision=lax.Precision.HIGH
     )
     return (input_grad[None, None], own_momentum[None], outer_update[None])
 

time: 133 us -> 120 us (0.902)
  the two profiles are of different devices: /device:TPU:74 before, /device:TPU:50 now
where the time goes in v3:
time: 120 us
  blocking collectives  44.1 us (37%)
  starting transfers between devices  41.4 us (34%)
  waiting for transfers between devices  14.7 us (12%)
  Pallas kernels  10.8 us (9%)
  matrix products  4.19 us (3%)
  local copies, waits for them, and re-layouts  1.77 us (1%)
  between operations  1.68 us (1%)
    all_gather x1, blocking collectives, shards(): pair_sums = lax.all_gather(pair_sums, 'island')  30.6 us
    all_gather x1, blocking collectives, shards(): line_keys = lax.all_gather(sent_keys, 'fsdp', axis_index_groups=x_lines)  13.5 us
    ppermute x3, starting transfers between devices, shards(): parts[turn] = lax.ppermute(parts[turn], 'fsdp', path)  9.94 us
    all_to_all x1, starting transfers between devices, shards(): pieces = lax.all_to_all(pieces, 'section', 0, 0)  8.95 us
    all_to_all x1, starting transfers between devices, shards(): pieces = lax.all_to_all(sums, 'section', 0, 0)  7.84 us
    ppermute x1, starting transfers between devices, exchange(): lax.ppermute(rows.astype(jnp.bfloat16), 'island', path).astype(jnp.float32)  6.08 us
    ppermute x1, waiting for transfers between devices, exchange(): lax.ppermute(rows.astype(jnp.bfloat16), 'island', path).astype(jnp.float32)  5.16 us
    all_to_all x1, waiting for transfers between devices, shards(): back = lax.all_to_all(back, 'fsdp', 0, 0, axis_index_groups=x_lines)  5.06 us
  transfers between devices with their start and end apart: 9, of which 4 were waited for; matrix products, arithmetic and copies ran while one was open for 4% of the time, Pallas kernels for 3%

profile of v3, /device:TPU:50, one launch (start us, length us, event | category | flops | bytes accessed | tf_op | source)
XLA Modules:
  0.0 119.6 jit_solution(6302883995982556816)
XLA Ops:
  0.7 3.1 %prepare.1 = (bf16[4,128,512]{2,1,0:T(8,128)(2,1)}, bf16[1024,512]{1,0:T(8,128)(2,1)}) custom-call(s32[1]{0:T(128)} %bitcast.1.core_ref, bf16[128,4096]{1,0:T(8,128)(2,1)} %bitcast.45, f32[1,4096]{1,0:T(1,128)} %gain_ref.3, bf16[512,512]{1,0:T(8,128)(2,1)} %bitcast.49), custom_call_target="tpu_custom_call" | custom-call | tf_op jit(solution)/shard_map/prepare/pallas_call | solution.py:214
  3.7 2.1 %collective-permute-start = (bf16[1024,512]{1,0:T(8,128)(2,1)}, bf16[1024,512]{1,0:T(8,128)(2,1)S(1)}, u32[]{:S(2)}, u32[]{:S(2)}) collective-permute-start(bf16[1024,512]{1,0:T(8,128)(2,1)} %get-tuple-element.26), channel_id=1, source_target_pairs={{0,1},{1,0},{2,3},{3,2},{4,5},{5,4},{6,7},{7,6},{8,9},{9,8},{10,11... | collective-permute-start | bytes 3145736 | tf_op jit(solution)/shard_map/ppermute | solution.py:376
  5.8 13.5 %all-gather = bf16[512,512]{1,0:T(8,128)(2,1)S(1)} all-gather(bf16[128,512]{1,0:T(8,128)(2,1)S(1)} %bitcast.53), channel_id=2, replica_groups={{0,2,4,6},{1,3,5,7},{8,10,12,14},{9,11,13,15},{16,18,20,22},{17,19,21,2..., dimensions={0}, use_global_device_ids=true | all-gather | bytes 655360 | tf_op jit(solution)/shard_map/all_gather | solution.py:377
  19.3 1.5 %key_back_columns.1 = bf16[4,128,1024]{2,1,0:T(8,128)(2,1)} custom-call(s32[1]{0:T(128)} %bitcast.1.core_ref, bf16[4,128,512]{2,1,0:T(8,128)(2,1)S(1)} %bitcast.47, bf16[512,512]{1,0:T(8,128)(2,1)S(1)} %bitcast.50, bf16[1024,512]{1,0:T(8,128)(2,1)S(1)} %collective-permute-done.other_ref), custom_call_target="tpu_custom_call" | custom-call | tf_op jit(solution)/shard_map/key_back_columns/pallas_call | solution.py:122
  20.9 4.5 %all-to-all-start = ((bf16[4,128,1024]{2,1,0:T(8,128)(2,1)}), bf16[4,128,1024]{2,1,0:T(8,128)(2,1)S(1)}, u32[]{:S(2)}, u32[]{:S(2)}) async-start(bf16[4,128,1024]{2,1,0:T(8,128)(2,1)} %key_back_columns.1), calls=%async_computation | async-start | bytes 2097152 | tf_op jit(solution)/shard_map/all_to_all | solution.py:380
  26.7 2.1 %collective-permute-start.1 = (bf16[4,128,256]{2,1,0:T(8,128)(2,1)S(1)}, bf16[4,128,256]{2,1,0:T(8,128)(2,1)S(1)}, u32[]{:S(2)}, u32[]{:S(2)}) collective-permute-start(bf16[4,128,256]{2,1,0:T(8,128)(2,1)S(1)} %convolution_convert_fusion.own_keys), channel_id=1, source_target_pairs={{0,1},{1,0},{2,3},{3,2},{4,5},{5,4},{6,7},{7,6},{8,9},{9,8},{10,11... | collective-permute-start | bytes 786440 | tf_op jit(solution)/shard_map/ppermute | solution.py:389
  28.8 2.3 %pair_columns.1 = (bf16[2,128,512]{2,1,0:T(8,128)(2,1)}, bf16[2,128,512]{2,1,0:T(8,128)(2,1)}, bf16[2,128,512]{2,1,0:T(8,128)(2,1)}, bf16[2,128,512]{2,1,0:T(8,128)(2,1)}) custom-call(s32[1]{0:T(128)} %bitcast.7.chip_ref, bf16[4,128,512]{2,1,0:T(8,128)(2,1)} %get-tuple-element.29.own_ref, bf16[1024,512]{1,0:T(8,128)(2,1)S(1)} %copy-done.3), custom_call_target="tpu_custom_call" | custom-call | tf_op jit(solution)/shard_map/pair_columns/pallas_call | solution.py:261
  31.8 5.1 %all-to-all-done.back_ref = bf16[4,128,1024]{2,1,0:T(8,128)(2,1)S(1)} async-done(((bf16[4,128,1024]{2,1,0:T(8,128)(2,1)}), bf16[4,128,1024]{2,1,0:T(8,128)(2,1)S(1)}, u32[]{:S(2)}, u32[]{:S(2)}) %all-to-all-start) | async-done | bytes 1048608 | tf_op jit(solution)/shard_map/all_to_all | solution.py:380
  36.9 2.1 %branch_pieces.1 = bf16[16,8,4096]{2,1,0:T(8,128)(2,1)} custom-call(bf16[128,4096]{1,0:T(8,128)(2,1)S(1)} %bitcast.46, bf16[4,128,1024]{2,1,0:T(8,128)(2,1)S(1)} %all-to-all-done.back_ref, f32[1,4096]{1,0:T(1,128)S(1)} %copy-done.8), custom_call_target="tpu_custom_call" | custom-call | tf_op jit(solution)/shard_map/branch_pieces/pallas_call | solution.py:347
  39.0 9.0 %all-to-all-start.1 = ((bf16[16,8,4096]{2,1,0:T(8,128)(2,1)}), bf16[16,8,4096]{2,1,0:T(8,128)(2,1)S(1)}, u32[]{:S(2)}, u32[]{:S(2)}) async-start(bf16[16,8,4096]{2,1,0:T(8,128)(2,1)} %branch_pieces.1), calls=%async_computation.1 | async-start | bytes 2097152 | tf_op jit(solution)/shard_map/all_to_all | solution.py:395
  48.0 2.1 %collective-permute-start.2 = (bf16[2,128,512]{2,1,0:T(8,128)(2,1)S(1)}, bf16[2,128,512]{2,1,0:T(8,128)(2,1)S(1)}, u32[]{:S(2)}, u32[]{:S(2)}) collective-permute-start(bf16[2,128,512]{2,1,0:T(8,128)(2,1)S(1)} %copy-done.13), channel_id=1, source_target_pairs={{0,2},{1,3},{2,4},{3,5},{4,6},{5,7},{6,0},{7,1},{8,10},{9,11},{10,... | collective-permute-start | bytes 786440 | tf_op jit(solution)/shard_map/ppermute | solution.py:399
  50.1 5.4 %collective-permute-start.3 = (bf16[2,128,512]{2,1,0:T(8,128)(2,1)S(1)}, bf16[2,128,512]{2,1,0:T(8,128)(2,1)S(1)}, u32[]{:S(2)}, u32[]{:S(2)}) collective-permute-start(bf16[2,128,512]{2,1,0:T(8,128)(2,1)S(1)} %copy-done.12), channel_id=1, source_target_pairs={{0,4},{1,5},{2,6},{3,7},{4,0},{5,1},{6,2},{7,3},{8,12},{9,13},{10,... | collective-permute-start | bytes 786440 | tf_op jit(solution)/shard_map/ppermute | solution.py:399
  55.5 2.5 %collective-permute-start.4 = (bf16[2,128,512]{2,1,0:T(8,128)(2,1)S(1)}, bf16[2,128,512]{2,1,0:T(8,128)(2,1)S(1)}, u32[]{:S(2)}, u32[]{:S(2)}) collective-permute-start(bf16[2,128,512]{2,1,0:T(8,128)(2,1)S(1)} %copy-done.11), channel_id=1, source_target_pairs={{0,6},{1,7},{2,0},{3,1},{4,2},{5,3},{6,4},{7,5},{8,14},{9,15},{10,... | collective-permute-start | bytes 786440 | tf_op jit(solution)/shard_map/ppermute | solution.py:399
  58.0 1.3 %fusion.1.drift_ref = f32[256,512]{1,0:T(8,128)S(1)} fusion(f32[1,1,512,512]{3,2,1,0:T(8,128)S(1)} %copy-done, s32[]{:T(128)} %bitcast.5, s32[512]{0:T(512)S(1)} %iota_multiply_fusion), kind=kOutput, calls=%fused_computation.3 | convolution fusion | flops 404750336 | bytes 1574916 | tf_op jit(solution)/shard_map/kr,dk->rd/dot_general | solution.py:400
  59.3 1.3 %collective-permute-done.3.part2 = bf16[2,128,512]{2,1,0:T(8,128)(2,1)S(1)} collective-permute-done((bf16[2,128,512]{2,1,0:T(8,128)(2,1)S(1)}, bf16[2,128,512]{2,1,0:T(8,128)(2,1)S(1)}, u32[]{:S(2)}, u32[]{:S(2)}) %collective-permute-start.3) | collective-permute-done | bytes 262176 | tf_op jit(solution)/shard_map/ppermute | solution.py:399
  60.7 3.1 %collective-permute-done.4.part3 = bf16[2,128,512]{2,1,0:T(8,128)(2,1)S(1)} collective-permute-done((bf16[2,128,512]{2,1,0:T(8,128)(2,1)S(1)}, bf16[2,128,512]{2,1,0:T(8,128)(2,1)S(1)}, u32[]{:S(2)}, u32[]{:S(2)}) %collective-permute-start.4) | collective-permute-done | bytes 262176 | tf_op jit(solution)/shard_map/ppermute | solution.py:399
  63.8 0.7 factor_columns.1
  64.6 6.1 %collective-permute-start.5 = (bf16[128,512]{1,0:T(8,128)(2,1)S(1)}, bf16[128,512]{1,0:T(8,128)(2,1)S(1)}, u32[]{:S(2)}, u32[]{:S(2)}) collective-permute-start(bf16[128,512]{1,0:T(8,128)(2,1)S(1)} %pad_maximum_fusion), channel_id=1, source_target_pairs={{0,128},{128,0},{256,384},{384,256},{1,129},{129,1},{257,385},{385... | collective-permute-start | bytes 393224 | tf_op jit(solution)/shard_map/ppermute | solution.py:411
  70.7 5.2 %collective-permute-done.5 = bf16[128,512]{1,0:T(8,128)(2,1)S(1)} collective-permute-done((bf16[128,512]{1,0:T(8,128)(2,1)S(1)}, bf16[128,512]{1,0:T(8,128)(2,1)S(1)}, u32[]{:S(2)}, u32[]{:S(2)}) %collective-permute-start.5) | collective-permute-done | bytes 131104 | tf_op jit(solution)/shard_map/ppermute | solution.py:411
  76.0 1.0 suffix_sums.1
  77.0 7.8 %all-to-all-start.2 = ((bf16[16,8,4096]{2,1,0:T(8,128)(2,1)}), bf16[16,8,4096]{2,1,0:T(8,128)(2,1)S(1)}, u32[]{:S(2)}, u32[]{:S(2)}) async-start(bf16[16,8,4096]{2,1,0:T(8,128)(2,1)} %suffix_sums.1), calls=%async_computation.2 | async-start | bytes 2097152 | tf_op jit(solution)/shard_map/all_to_all | solution.py:417
  84.9 30.6 %all_gather.12 = bf16[4,2,64,512]{3,2,1,0:T(8,128)(2,1)S(1)} all-gather(bf16[1,2,64,512]{3,2,1,0:T(8,128)(2,1)S(1)} %pad_maximum_fusion.1), channel_id=1, replica_groups=mesh['island'=4,'section'=16,'fsdp'=8] {'island'}, dimensions={0}, use_global_device_ids=true | all-gather | bytes 655360 | tf_op jit(solution)/shard_map/all_gather | solution.py:423
  115.7 2.3 %fusion = f32[1,512,512]{2,1,0:T(8,128)} fusion(f32[64,512]{1,0:T(8,128)S(1)} %get-tuple-element.48, f32[64,512]{1,0:T(8,128)S(1)} %get-tuple-element.47, f32[64,512]{1,0:T(8,128)S(1)} %get-tuple-element.46, f32[64,512]{1,0:T(8,128)S(1)} %get-tuple-element.45, s32[]{:T(128)} %bitcast.5, s32[512]{0:T(512)S(1)} %iota_multiply_fusion), kind=kOutput, calls=%fused_computation.1 | convolution fusion | flops 405405696 | bytes 1574916 | tf_op jit(solution)/shard_map/rd,kr->dk/dot_general | solution.py:429
  118.7 1.0 copy.12
  (45 shorter events, 2.4 us)
Async XLA Ops:
  0.6 57.4 %copy-start = (f32[1,1,512,512]{3,2,1,0:T(8,128)S(1)}, f32[1,1,512,512]{3,2,1,0:T(8,128)}, u32[]{:S(2)}) copy-start(f32[1,1,512,512]{3,2,1,0:T(8,128)} %param.11) | copy-start | bytes 3145732
  0.7 5.1 %copy-start.10 = (bf16[1,1,128,512]{3,2,1,0:T(8,128)(2,1)S(1)}, bf16[1,1,128,512]{3,2,1,0:T(8,128)(2,1)}, u32[]{:S(2)}) copy-start(bf16[1,1,128,512]{3,2,1,0:T(8,128)(2,1)} %param.9) | copy-start | bytes 393220
  3.7 15.6 %copy-start.4 = (bf16[1,1,512,512]{3,2,1,0:T(8,128)(2,1)S(1)}, bf16[1,1,512,512]{3,2,1,0:T(8,128)(2,1)}, u32[]{:S(2)}) copy-start(bf16[1,1,512,512]{3,2,1,0:T(8,128)(2,1)} %param.10) | copy-start | bytes 1572868
  3.7 15.6 %collective-permute-start = (bf16[1024,512]{1,0:T(8,128)(2,1)}, bf16[1024,512]{1,0:T(8,128)(2,1)S(1)}, u32[]{:S(2)}, u32[]{:S(2)}) collective-permute-start(bf16[1024,512]{1,0:T(8,128)(2,1)} %get-tuple-element.26), channel_id=1, source_target_pairs={{0,1},{1,0},{2,3},{3,2},{4,5},{5,4},{6,7},{7,6},{8,9},{9,8},{10,11... | collective-permute-start | bytes 3145736 | tf_op jit(solution)/shard_map/ppermute | solution.py:376
  19.3 1.6 %copy-start.2 = (bf16[1024,512]{1,0:T(8,128)(2,1)}, bf16[1024,512]{1,0:T(8,128)(2,1)S(1)}, u32[]{:S(2)}) copy-start(bf16[1024,512]{1,0:T(8,128)(2,1)S(1)} %collective-permute-done.other_ref) | copy-start | bytes 3145732
  20.9 16.0 %all-to-all-start = ((bf16[4,128,1024]{2,1,0:T(8,128)(2,1)}), bf16[4,128,1024]{2,1,0:T(8,128)(2,1)S(1)}, u32[]{:S(2)}, u32[]{:S(2)}) async-start(bf16[4,128,1024]{2,1,0:T(8,128)(2,1)} %key_back_columns.1), calls=%async_computation | async-start | bytes 2097152 | tf_op jit(solution)/shard_map/all_to_all | solution.py:380
  26.0 2.7 %copy-start.3 = (bf16[1024,512]{1,0:T(8,128)(2,1)S(1)}, bf16[1024,512]{1,0:T(8,128)(2,1)}, u32[]{:S(2)}) copy-start(bf16[1024,512]{1,0:T(8,128)(2,1)} %copy-done.2) | copy-start | bytes 3145732
  26.7 10.2 %copy-start.1 = (bf16[1,1,128,4096]{3,2,1,0:T(8,128)(2,1)S(1)}, bf16[1,1,128,4096]{3,2,1,0:T(8,128)(2,1)}, u32[]{:S(2)}) copy-start(bf16[1,1,128,4096]{3,2,1,0:T(8,128)(2,1)} %param.7) | copy-start | bytes 3145732
  26.7 4.4 %collective-permute-start.1 = (bf16[4,128,256]{2,1,0:T(8,128)(2,1)S(1)}, bf16[4,128,256]{2,1,0:T(8,128)(2,1)S(1)}, u32[]{:S(2)}, u32[]{:S(2)}) collective-permute-start(bf16[4,128,256]{2,1,0:T(8,128)(2,1)S(1)} %convolution_convert_fusion.own_keys), channel_id=1, source_target_pairs={{0,1},{1,0},{2,3},{3,2},{4,5},{5,4},{6,7},{7,6},{8,9},{9,8},{10,11... | collective-permute-start | bytes 786440 | tf_op jit(solution)/shard_map/ppermute | solution.py:389
  28.8 8.1 %copy-start.8 = (f32[1,4096]{1,0:T(1,128)S(1)}, f32[1,4096]{1,0:T(1,128)}, u32[]{:S(2)}) copy-start(f32[1,4096]{1,0:T(1,128)} %gain_ref.3) | copy-start | bytes 49156
  31.1 0.7 copy-start.5
  39.0 9.0 %copy-start.13 = (bf16[2,128,512]{2,1,0:T(8,128)(2,1)S(1)}, bf16[2,128,512]{2,1,0:T(8,128)(2,1)}, u32[]{:S(2)}) copy-start(bf16[2,128,512]{2,1,0:T(8,128)(2,1)} %get-tuple-element.39) | copy-start | bytes 786436
  39.0 11.1 %copy-start.12 = (bf16[2,128,512]{2,1,0:T(8,128)(2,1)S(1)}, bf16[2,128,512]{2,1,0:T(8,128)(2,1)}, u32[]{:S(2)}) copy-start(bf16[2,128,512]{2,1,0:T(8,128)(2,1)} %get-tuple-element.40) | copy-start | bytes 786436
  39.0 16.5 %copy-start.11 = (bf16[2,128,512]{2,1,0:T(8,128)(2,1)S(1)}, bf16[2,128,512]{2,1,0:T(8,128)(2,1)}, u32[]{:S(2)}) copy-start(bf16[2,128,512]{2,1,0:T(8,128)(2,1)} %get-tuple-element.41) | copy-start | bytes 786436
  39.0 36.9 %all-to-all-start.1 = ((bf16[16,8,4096]{2,1,0:T(8,128)(2,1)}), bf16[16,8,4096]{2,1,0:T(8,128)(2,1)S(1)}, u32[]{:S(2)}, u32[]{:S(2)}) async-start(bf16[16,8,4096]{2,1,0:T(8,128)(2,1)} %branch_pieces.1), calls=%async_computation.1 | async-start | bytes 2097152 | tf_op jit(solution)/shard_map/all_to_all | solution.py:395
  48.0 15.8 %copy-start.6 = (bf16[4,128,256]{2,1,0:T(8,128)(2,1)S(1)}, bf16[4,128,256]{2,1,0:T(8,128)(2,1)}, u32[]{:S(2)}) copy-start(bf16[4,128,256]{2,1,0:T(8,128)(2,1)} %copy-done.5) | copy-start | bytes 786436
  48.0 15.8 %copy-start.7 = (bf16[2,128,512]{2,1,0:T(8,128)(2,1)S(1)}, bf16[2,128,512]{2,1,0:T(8,128)(2,1)}, u32[]{:S(2)}) copy-start(bf16[2,128,512]{2,1,0:T(8,128)(2,1)} %get-tuple-element.38.part0) | copy-start | bytes 786436
  48.0 11.3 %collective-permute-start.2 = (bf16[2,128,512]{2,1,0:T(8,128)(2,1)S(1)}, bf16[2,128,512]{2,1,0:T(8,128)(2,1)S(1)}, u32[]{:S(2)}, u32[]{:S(2)}) collective-permute-start(bf16[2,128,512]{2,1,0:T(8,128)(2,1)S(1)} %copy-done.13), channel_id=1, source_target_pairs={{0,2},{1,3},{2,4},{3,5},{4,6},{5,7},{6,0},{7,1},{8,10},{9,11},{10,... | collective-permute-start | bytes 786440 | tf_op jit(solution)/shard_map/ppermute | solution.py:399
  50.1 10.6 %collective-permute-start.3 = (bf16[2,128,512]{2,1,0:T(8,128)(2,1)S(1)}, bf16[2,128,512]{2,1,0:T(8,128)(2,1)S(1)}, u32[]{:S(2)}, u32[]{:S(2)}) collective-permute-start(bf16[2,128,512]{2,1,0:T(8,128)(2,1)S(1)} %copy-done.12), channel_id=1, source_target_pairs={{0,4},{1,5},{2,6},{3,7},{4,0},{5,1},{6,2},{7,3},{8,12},{9,13},{10,... | collective-permute-start | bytes 786440 | tf_op jit(solution)/shard_map/ppermute | solution.py:399
  55.5 8.3 %collective-permute-start.4 = (bf16[2,128,512]{2,1,0:T(8,128)(2,1)S(1)}, bf16[2,128,512]{2,1,0:T(8,128)(2,1)S(1)}, u32[]{:S(2)}, u32[]{:S(2)}) collective-permute-start(bf16[2,128,512]{2,1,0:T(8,128)(2,1)S(1)} %copy-done.11), channel_id=1, source_target_pairs={{0,6},{1,7},{2,0},{3,1},{4,2},{5,3},{6,4},{7,5},{8,14},{9,15},{10,... | collective-permute-start | bytes 786440 | tf_op jit(solution)/shard_map/ppermute | solution.py:399
  64.6 11.3 %collective-permute-start.5 = (bf16[128,512]{1,0:T(8,128)(2,1)S(1)}, bf16[128,512]{1,0:T(8,128)(2,1)S(1)}, u32[]{:S(2)}, u32[]{:S(2)}) collective-permute-start(bf16[128,512]{1,0:T(8,128)(2,1)S(1)} %pad_maximum_fusion), channel_id=1, source_target_pairs={{0,128},{128,0},{256,384},{384,256},{1,129},{129,1},{257,385},{385... | collective-permute-start | bytes 393224 | tf_op jit(solution)/shard_map/ppermute | solution.py:411
  77.0 7.9 %copy-start.9 = (f32[1,64,512]{2,1,0:T(8,128)S(1)}, f32[1,64,512]{2,1,0:T(8,128)}, u32[]{:S(2)}) copy-start(f32[1,64,512]{2,1,0:T(8,128)} %param.12) | copy-start | bytes 393220
  77.0 41.6 %all-to-all-start.2 = ((bf16[16,8,4096]{2,1,0:T(8,128)(2,1)}), bf16[16,8,4096]{2,1,0:T(8,128)(2,1)S(1)}, u32[]{:S(2)}, u32[]{:S(2)}) async-start(bf16[16,8,4096]{2,1,0:T(8,128)(2,1)} %suffix_sums.1), calls=%async_computation.2 | async-start | bytes 2097152 | tf_op jit(solution)/shard_map/all_to_all | solution.py:417

commit v4 on v3

--- a/solution.py
+++ b/solution.py
@@ -134,102 +134,85 @@
 
 
 def prepare_kernel(
-    core_ref,
-    hidden_ref,
-    gain_ref,
-    weight_ref,
-    own_ref,
-    swap_ref,
-    held,
-    gain,
-    outs,
-    weight,
-    held_sems,
-    out_sems,
+    core_ref, hidden_ref, gain_ref, weight_ref, own_ref, swap_ref, held, gain, out, held_sems, out_sems
 ):
     tokens, width = hidden_ref.shape
     chips, _, slice_width = own_ref.shape
-    chunks = out_sems.shape[1]
+    chunks = held_sems.shape[0] - 2
+    rows = tokens // chunks
     core = core_ref[0]
-    rows = tokens // chunks
 
     def arrival(chunk):
         lines = pl.ds(chunk * rows, rows)
         return pltpu.make_async_copy(hidden_ref.at[lines], held.at[lines], held_sems.at[chunk])
 
-    def departures(chunk):
+    def departure(chunk):
         lines = pl.ds(chunk * rows, rows)
-        for chip in range(chips):
-            below = pl.ds(slice_width + chip * tokens + chunk * rows, rows)
-            for side, place in enumerate((own_ref.at[chip, lines], swap_ref.at[below])):
-                yield pltpu.make_async_copy(
-                    outs.at[side, chip, lines], place, out_sems.at[side, chunk, chip]
-                )
+        return pltpu.make_async_copy(out.at[:, lines], own_ref.at[:, lines], out_sems.at[chunk])
 
     gain_in = pltpu.make_async_copy(gain_ref, gain, held_sems.at[chunks])
-    weight_in = pltpu.make_async_copy(weight_ref, weight, held_sems.at[chunks + 1])
-    weight_out = pltpu.make_async_copy(
-        weight, swap_ref.at[pl.ds(0, slice_width)], held_sems.at[chunks + 2]
+    weight_in = pltpu.make_async_copy(
+        weight_ref, swap_ref.at[pl.ds(0, chips)], held_sems.at[chunks + 1]
     )
     arrival(0).start()
     gain_in.start()
     for chunk in range(1, chunks):
         arrival(chunk).start()
     weight_in.start()
-    gain_in.wait()
     for chunk in range(chunks):
         arrival(chunk).wait()
         lines = pl.ds(chunk * rows, rows)
         squares = [jnp.zeros((rows, 128), jnp.float32)] * 2
-        for column in range(0, width // 128):
+        for column in range(width // 128):
             value = held[lines, column * 128 : column * 128 + 128].astype(jnp.float32)
             squares[column % 2] = squares[column % 2] + value * value
         total = jnp.sum(squares[0] + squares[1], -1, keepdims=True)
         recip = lax.rsqrt(total / width + 1e-05)
+        if chunk == 0:
+            gain_in.wait()
         for chip in range(chips):
-            for side, place in enumerate((core, 1 - core)):
+            for to_ref, at, place in ((out, chip, core), (swap_ref, chips + chip, 1 - core)):
                 first = pl.multiple_of((CORES * chip + place) * slice_width, slice_width)
                 for column in range(0, slice_width, 128):
                     span = pl.ds(pl.multiple_of(first + column, 128), 128)
                     value = held[lines, span].astype(jnp.float32) * recip
-                    normed = (value * gain[:, span]).astype(outs.dtype)
-                    outs[side, chip, lines, column : column + 128] = normed
-        for copy in departures(chunk):
-            copy.start()
-        if chunk == 0:
-            weight_in.wait()
-            weight_out.start()
-    weight_out.wait()
+                    normed = (value * gain[:, span]).astype(to_ref.dtype)
+                    to_ref[at, lines, column : column + 128] = normed
+        departure(chunk).start()
+    weight_in.wait()
     for chunk in range(chunks):
-        for copy in departures(chunk):
-            copy.wait()
+        departure(chunk).wait()
 
 
 def prepare(core, hidden, gain_row, weight):
     tokens, width = hidden.shape
     slice_width, key_width = weight.shape
     chips = width // slice_width // CORES
-    chunks = 4
-    columns = (chips, tokens, slice_width)
-    return pl.pallas_call(
+    chunks = 2
+    own, swapped = pl.pallas_call(
         prepare_kernel,
         out_shape=(
-            pltpu.HBM(columns, jnp.bfloat16),
-            pltpu.HBM((slice_width + chips * tokens, key_width), jnp.bfloat16),
+            pltpu.HBM((chips, tokens, slice_width), jnp.bfloat16),
+            pltpu.VMEM((2 * chips, tokens, slice_width), jnp.bfloat16),
         ),
         in_specs=[pl.BlockSpec(memory_space=pltpu.SMEM)] + [whole_hbm()] * 3,
-        out_specs=(whole_hbm(),) * 2,
+        out_specs=(whole_hbm(), whole_vmem()),
         scratch_shapes=[
             pltpu.VMEM(hidden.shape, hidden.dtype),
             pltpu.VMEM(gain_row.shape, gain_row.dtype),
-            pltpu.VMEM((CORES, *columns), jnp.bfloat16),
-            pltpu.VMEM(weight.shape, weight.dtype),
-            pltpu.SemaphoreType.DMA((chunks + 3,)),
-            pltpu.SemaphoreType.DMA((CORES, chunks, chips)),
+            pltpu.VMEM((chips, tokens, slice_width), jnp.bfloat16),
+            pltpu.SemaphoreType.DMA((chunks + 2,)),
+            pltpu.SemaphoreType.DMA((chunks,)),
         ],
         compiler_params=kernel_params(),
         name="prepare",
-    )(core.reshape(1), in_hbm(hidden), in_hbm(gain_row), in_hbm(weight))
+    )(
+        core.reshape(1),
+        in_hbm(hidden),
+        in_hbm(gain_row),
+        in_hbm(weight.reshape(chips, tokens, key_width)),
+    )
+    return own, swapped.reshape(2 * chips * tokens, slice_width)
 
 
 def pair_kernel(chip_ref, own_ref, other_ref, *refs):
@@ -261,7 +244,7 @@
     return pl.pallas_call(
         pair_kernel,
         out_shape=(pltpu.HBM(shape, own_normed.dtype),) * chips,
-        in_specs=[pl.BlockSpec(memory_space=pltpu.SMEM), whole_hbm(), anywhere()],
+        in_specs=[pl.BlockSpec(memory_space=pltpu.SMEM), anywhere(), anywhere()],
         out_specs=(whole_hbm(),) * chips,
         scratch_shapes=[
             pltpu.VMEM((chips, *shape), own_normed.dtype),
@@ -270,7 +253,7 @@
         ],
         compiler_params=kernel_params(),
         name="pair_columns",
-    )(chip.reshape(1), in_hbm(own_normed), arrived)
+    )(chip.reshape(1), own_normed, arrived)
 
 
 def factor_kernel(chip_ref, own_keys, other_keys, drift_ref, part0, part1, part2, part3, sum_ref):
@@ -305,39 +288,38 @@
     rows = 16
     count = pieces_ref.shape[1]
     each = rows // count
+    columns = [(chip, column) for chip in range(chips) for column in range(0, span, 128)]
 
     def departure(place):
         run = pl.ds(place * each, each)
         return pltpu.make_async_copy(out.at[run], pieces_ref.at[run], out_sem)
 
-    def group(place, carry):
-        lines = pl.ds(pl.multiple_of(place * rows, rows), rows)
-        squares = jnp.zeros((rows, 128), jnp.float32)
-        cross = jnp.zeros((rows, 128), jnp.float32)
-        for chip in range(chips):
-            for column in range(0, span, 128):
-                at = chip * span + column
-                value = hidden_ref[lines, at : at + 128].astype(jnp.float32)
-                back = back_ref[chip, lines, column : column + 128].astype(jnp.float32)
-                squares = squares + value * value
-                cross = cross + value * (back * gain_ref[:, at : at + 128])
-        recip = lax.rsqrt(jnp.sum(squares, -1, keepdims=True) / width + 1e-05)
-        mean = jnp.sum(cross, -1, keepdims=True) * recip / width
+    for place in range(tokens // rows):
+        lines = pl.ds(place * rows, rows)
+
+        def tile(chip, column, lines=lines):
+            at = chip * span + column
+            value = hidden_ref[lines, at : at + 128].astype(jnp.float32)
+            back = back_ref[chip, lines, column : column + 128].astype(jnp.float32)
+            return at, value, back * gain_ref[:, at : at + 128]
+
+        squares = [jnp.zeros((rows, 128), jnp.float32)] * 2
+        cross = [jnp.zeros((rows, 128), jnp.float32)] * 2
+        for index, (chip, column) in enumerate(columns):
+            _, value, scaled = tile(chip, column)
+            squares[index % 2] = squares[index % 2] + value * value
+            cross[index % 2] = cross[index % 2] + value * scaled
+        total = jnp.sum(squares[0] + squares[1], -1, keepdims=True)
+        recip = lax.rsqrt(total / width + 1e-05)
+        mean = jnp.sum(cross[0] + cross[1], -1, keepdims=True) * recip / width
         share = recip * recip * mean
-        for chip in range(chips):
-            for column in range(0, span, 128):
-                at = chip * span + column
-                value = hidden_ref[lines, at : at + 128].astype(jnp.float32)
-                back = back_ref[chip, lines, column : column + 128].astype(jnp.float32)
-                branch = recip * (back * gain_ref[:, at : at + 128]) - share * value
-                branch = branch.astype(out.dtype)
-                for part in range(each):
-                    lines_of = branch[part * count : (part + 1) * count]
-                    out[place * each + part, :, at : at + 128] = lines_of
+        for chip, column in columns:
+            at, value, scaled = tile(chip, column)
+            branch = (recip * scaled - share * value).astype(out.dtype)
+            for part in range(each):
+                lines_of = branch[part * count : (part + 1) * count]
+                out[place * each + part, :, at : at + 128] = lines_of
         departure(place).start()
-        return carry
-
-    lax.fori_loop(0, tokens // rows, group, 0)
     pltpu.make_async_copy(out, pieces_ref, out_sem).wait()
 
 

time: 120 us -> 117 us (0.975)
  the two profiles are of different devices: /device:TPU:50 before, /device:TPU:104 now
where the time goes in v4:
time: 117 us; the launch traced here: 116 us
  blocking collectives  42.9 us (37%)
  starting transfers between devices  39.8 us (34%)
  waiting for transfers between devices  15 us (13%)
  Pallas kernels  9.98 us (9%)
  matrix products  4.19 us (4%)
  local copies, waits for them, and re-layouts  1.77 us (2%)
  between operations  1.69 us (1%)
    all_gather x1, blocking collectives, shards(): pair_sums = lax.all_gather(pair_sums, 'island')  29.5 us
    all_gather x1, blocking collectives, shards(): line_keys = lax.all_gather(sent_keys, 'fsdp', axis_index_groups=x_lines)  13.4 us
    ppermute x3, starting transfers between devices, shards(): parts[turn] = lax.ppermute(parts[turn], 'fsdp', path)  9.11 us
    all_to_all x1, starting transfers between devices, shards(): pieces = lax.all_to_all(sums, 'section', 0, 0)  8.27 us
    all_to_all x1, starting transfers between devices, shards(): pieces = lax.all_to_all(pieces, 'section', 0, 0)  8.16 us
    all_to_all x1, waiting for transfers between devices, shards(): back = lax.all_to_all(back, 'fsdp', 0, 0, axis_index_groups=x_lines)  6.3 us
    ppermute x1, starting transfers between devices, exchange(): lax.ppermute(rows.astype(jnp.bfloat16), 'island', path).astype(jnp.float32)  6.04 us
    ppermute x3, waiting for transfers between devices, shards(): parts[turn] = lax.ppermute(parts[turn], 'fsdp', path)  4.8 us
  transfers between devices with their start and end apart: 9, of which 4 were waited for; matrix products, arithmetic and copies ran while one was open for 4% of the time, Pallas kernels for 3%

profile of v4, /device:TPU:104, one launch (start us, length us, event | category | flops | bytes accessed | tf_op | source)
XLA Modules:
  0.0 116.3 jit_solution(6979917477710922854)
XLA Ops:
  0.7 2.5 %prepare.1 = (bf16[4,128,512]{2,1,0:T(8,128)(2,1)}, bf16[8,128,512]{2,1,0:T(8,128)(2,1)S(1)}) custom-call(s32[1]{0:T(128)} %bitcast.1.core_ref, bf16[128,4096]{1,0:T(8,128)(2,1)} %bitcast.47, f32[1,4096]{1,0:T(1,128)} %gain_ref.3, bf16[4,128,512]{2,1,0:T(8,128)(2,1)} %bitcast.51), custom_call_target="tpu_custom_call" | custom-call | tf_op jit(solution)/shard_map/prepare/pallas_call | solution.py:192
  3.2 2.1 %collective-permute-start = (bf16[1024,512]{1,0:T(8,128)(2,1)S(1)}, bf16[1024,512]{1,0:T(8,128)(2,1)S(1)}, u32[]{:S(2)}, u32[]{:S(2)}) collective-permute-start(bf16[1024,512]{1,0:T(8,128)(2,1)S(1)} %bitcast.53), channel_id=1, source_target_pairs={{0,1},{1,0},{2,3},{3,2},{4,5},{5,4},{6,7},{7,6},{8,9},{9,8},{10,11... | collective-permute-start | bytes 3145736 | tf_op jit(solution)/shard_map/ppermute | solution.py:358
  5.3 13.4 %all-gather = bf16[512,512]{1,0:T(8,128)(2,1)S(1)} all-gather(bf16[128,512]{1,0:T(8,128)(2,1)S(1)} %bitcast.56), channel_id=2, replica_groups={{0,2,4,6},{1,3,5,7},{8,10,12,14},{9,11,13,15},{16,18,20,22},{17,19,21,2..., dimensions={0}, use_global_device_ids=true | all-gather | bytes 655360 | tf_op jit(solution)/shard_map/all_gather | solution.py:359
  18.7 1.5 %key_back_columns.1 = bf16[4,128,1024]{2,1,0:T(8,128)(2,1)} custom-call(s32[1]{0:T(128)} %bitcast.1.core_ref, bf16[4,128,512]{2,1,0:T(8,128)(2,1)S(1)} %bitcast.49, bf16[512,512]{1,0:T(8,128)(2,1)S(1)} %bitcast.52, bf16[1024,512]{1,0:T(8,128)(2,1)S(1)} %collective-permute-done.other_ref), custom_call_target="tpu_custom_call" | custom-call | tf_op jit(solution)/shard_map/key_back_columns/pallas_call | solution.py:122
  20.2 4.1 %all-to-all-start = ((bf16[4,128,1024]{2,1,0:T(8,128)(2,1)}), bf16[4,128,1024]{2,1,0:T(8,128)(2,1)S(1)}, u32[]{:S(2)}, u32[]{:S(2)}) async-start(bf16[4,128,1024]{2,1,0:T(8,128)(2,1)} %key_back_columns.1), calls=%async_computation | async-start | bytes 2097152 | tf_op jit(solution)/shard_map/all_to_all | solution.py:362
  25.7 2.1 %collective-permute-start.1 = (bf16[4,128,256]{2,1,0:T(8,128)(2,1)S(1)}, bf16[4,128,256]{2,1,0:T(8,128)(2,1)S(1)}, u32[]{:S(2)}, u32[]{:S(2)}) collective-permute-start(bf16[4,128,256]{2,1,0:T(8,128)(2,1)S(1)} %convolution_convert_fusion.own_keys), channel_id=1, source_target_pairs={{0,1},{1,0},{2,3},{3,2},{4,5},{5,4},{6,7},{7,6},{8,9},{9,8},{10,11... | collective-permute-start | bytes 786440 | tf_op jit(solution)/shard_map/ppermute | solution.py:371
  27.8 2.5 %pair_columns.1 = (bf16[2,128,512]{2,1,0:T(8,128)(2,1)}, bf16[2,128,512]{2,1,0:T(8,128)(2,1)}, bf16[2,128,512]{2,1,0:T(8,128)(2,1)}, bf16[2,128,512]{2,1,0:T(8,128)(2,1)}) custom-call(s32[1]{0:T(128)} %bitcast.9.chip_ref, bf16[4,128,512]{2,1,0:T(8,128)(2,1)S(1)} %copy-done.5, bf16[1024,512]{1,0:T(8,128)(2,1)S(1)} %copy-done.3), custom_call_target="tpu_custom_call" | custom-call | tf_op jit(solution)/shard_map/pair_columns/pallas_call | solution.py:244
  31.0 6.3 %all-to-all-done.back_ref = bf16[4,128,1024]{2,1,0:T(8,128)(2,1)S(1)} async-done(((bf16[4,128,1024]{2,1,0:T(8,128)(2,1)}), bf16[4,128,1024]{2,1,0:T(8,128)(2,1)S(1)}, u32[]{:S(2)}, u32[]{:S(2)}) %all-to-all-start) | async-done | bytes 1048608 | tf_op jit(solution)/shard_map/all_to_all | solution.py:362
  37.3 1.6 %branch_pieces.1 = bf16[16,8,4096]{2,1,0:T(8,128)(2,1)} custom-call(bf16[128,4096]{1,0:T(8,128)(2,1)S(1)} %bitcast.48, bf16[4,128,1024]{2,1,0:T(8,128)(2,1)S(1)} %all-to-all-done.back_ref, f32[1,4096]{1,0:T(1,128)S(1)} %copy-done.9), custom_call_target="tpu_custom_call" | custom-call | tf_op jit(solution)/shard_map/branch_pieces/pallas_call | solution.py:329
  39.0 8.2 %all-to-all-start.1 = ((bf16[16,8,4096]{2,1,0:T(8,128)(2,1)}), bf16[16,8,4096]{2,1,0:T(8,128)(2,1)S(1)}, u32[]{:S(2)}, u32[]{:S(2)}) async-start(bf16[16,8,4096]{2,1,0:T(8,128)(2,1)} %branch_pieces.1), calls=%async_computation.1 | async-start | bytes 2097152 | tf_op jit(solution)/shard_map/all_to_all | solution.py:377
  47.1 2.6 %collective-permute-start.2 = (bf16[2,128,512]{2,1,0:T(8,128)(2,1)S(1)}, bf16[2,128,512]{2,1,0:T(8,128)(2,1)S(1)}, u32[]{:S(2)}, u32[]{:S(2)}) collective-permute-start(bf16[2,128,512]{2,1,0:T(8,128)(2,1)S(1)} %copy-done.14), channel_id=1, source_target_pairs={{0,2},{1,3},{2,4},{3,5},{4,6},{5,7},{6,0},{7,1},{8,10},{9,11},{10,... | collective-permute-start | bytes 786440 | tf_op jit(solution)/shard_map/ppermute | solution.py:381
  49.8 4.0 %collective-permute-start.3 = (bf16[2,128,512]{2,1,0:T(8,128)(2,1)S(1)}, bf16[2,128,512]{2,1,0:T(8,128)(2,1)S(1)}, u32[]{:S(2)}, u32[]{:S(2)}) collective-permute-start(bf16[2,128,512]{2,1,0:T(8,128)(2,1)S(1)} %copy-done.13), channel_id=1, source_target_pairs={{0,4},{1,5},{2,6},{3,7},{4,0},{5,1},{6,2},{7,3},{8,12},{9,13},{10,... | collective-permute-start | bytes 786440 | tf_op jit(solution)/shard_map/ppermute | solution.py:381
  53.8 2.5 %collective-permute-start.4 = (bf16[2,128,512]{2,1,0:T(8,128)(2,1)S(1)}, bf16[2,128,512]{2,1,0:T(8,128)(2,1)S(1)}, u32[]{:S(2)}, u32[]{:S(2)}) collective-permute-start(bf16[2,128,512]{2,1,0:T(8,128)(2,1)S(1)} %copy-done.12), channel_id=1, source_target_pairs={{0,6},{1,7},{2,0},{3,1},{4,2},{5,3},{6,4},{7,5},{8,14},{9,15},{10,... | collective-permute-start | bytes 786440 | tf_op jit(solution)/shard_map/ppermute | solution.py:381
  56.3 1.3 %fusion.1.drift_ref = f32[256,512]{1,0:T(8,128)S(1)} fusion(f32[1,1,512,512]{3,2,1,0:T(8,128)S(1)} %copy-done, s32[]{:T(128)} %bitcast.7, s32[512]{0:T(512)S(1)} %iota_multiply_fusion), kind=kOutput, calls=%fused_computation.3 | convolution fusion | flops 404750336 | bytes 1574916 | tf_op jit(solution)/shard_map/kr,dk->rd/dot_general | solution.py:382
  57.6 2.3 %collective-permute-done.2.part1 = bf16[2,128,512]{2,1,0:T(8,128)(2,1)S(1)} collective-permute-done((bf16[2,128,512]{2,1,0:T(8,128)(2,1)S(1)}, bf16[2,128,512]{2,1,0:T(8,128)(2,1)S(1)}, u32[]{:S(2)}, u32[]{:S(2)}) %collective-permute-start.2) | collective-permute-done | bytes 262176 | tf_op jit(solution)/shard_map/ppermute | solution.py:381
  59.9 2.5 %collective-permute-done.4.part3 = bf16[2,128,512]{2,1,0:T(8,128)(2,1)S(1)} collective-permute-done((bf16[2,128,512]{2,1,0:T(8,128)(2,1)S(1)}, bf16[2,128,512]{2,1,0:T(8,128)(2,1)S(1)}, u32[]{:S(2)}, u32[]{:S(2)}) %collective-permute-start.4) | collective-permute-done | bytes 262176 | tf_op jit(solution)/shard_map/ppermute | solution.py:381
  62.4 0.7 factor_columns.1
  63.2 6.0 %collective-permute-start.5 = (bf16[128,512]{1,0:T(8,128)(2,1)S(1)}, bf16[128,512]{1,0:T(8,128)(2,1)S(1)}, u32[]{:S(2)}, u32[]{:S(2)}) collective-permute-start(bf16[128,512]{1,0:T(8,128)(2,1)S(1)} %pad_maximum_fusion), channel_id=1, source_target_pairs={{0,128},{128,0},{256,384},{384,256},{1,129},{129,1},{257,385},{385... | collective-permute-start | bytes 393224 | tf_op jit(solution)/shard_map/ppermute | solution.py:393
  69.3 3.9 %collective-permute-done.5 = bf16[128,512]{1,0:T(8,128)(2,1)S(1)} collective-permute-done((bf16[128,512]{1,0:T(8,128)(2,1)S(1)}, bf16[128,512]{1,0:T(8,128)(2,1)S(1)}, u32[]{:S(2)}, u32[]{:S(2)}) %collective-permute-start.5) | collective-permute-done | bytes 131104 | tf_op jit(solution)/shard_map/ppermute | solution.py:393
  73.2 1.0 suffix_sums.1
  74.3 8.3 %all-to-all-start.2 = ((bf16[16,8,4096]{2,1,0:T(8,128)(2,1)}), bf16[16,8,4096]{2,1,0:T(8,128)(2,1)S(1)}, u32[]{:S(2)}, u32[]{:S(2)}) async-start(bf16[16,8,4096]{2,1,0:T(8,128)(2,1)} %suffix_sums.1), calls=%async_computation.2 | async-start | bytes 2097152 | tf_op jit(solution)/shard_map/all_to_all | solution.py:399
  82.6 29.5 %all_gather.12 = bf16[4,2,64,512]{3,2,1,0:T(8,128)(2,1)S(1)} all-gather(bf16[1,2,64,512]{3,2,1,0:T(8,128)(2,1)S(1)} %pad_maximum_fusion.1), channel_id=1, replica_groups=mesh['island'=4,'section'=16,'fsdp'=8] {'island'}, dimensions={0}, use_global_device_ids=true | all-gather | bytes 655360 | tf_op jit(solution)/shard_map/all_gather | solution.py:405
  112.3 2.3 %fusion = f32[1,512,512]{2,1,0:T(8,128)} fusion(f32[64,512]{1,0:T(8,128)S(1)} %get-tuple-element.48, f32[64,512]{1,0:T(8,128)S(1)} %get-tuple-element.47, f32[64,512]{1,0:T(8,128)S(1)} %get-tuple-element.46, f32[64,512]{1,0:T(8,128)S(1)} %get-tuple-element.45, s32[]{:T(128)} %bitcast.7, s32[512]{0:T(512)S(1)} %iota_multiply_fusion), kind=kOutput, calls=%fused_computation.1 | convolution fusion | flops 405405696 | bytes 1574916 | tf_op jit(solution)/shard_map/rd,kr->dk/dot_general | solution.py:411
  115.3 1.0 copy.12
  (47 shorter events, 2.4 us)
Async XLA Ops:
  0.6 55.7 %copy-start = (f32[1,1,512,512]{3,2,1,0:T(8,128)S(1)}, f32[1,1,512,512]{3,2,1,0:T(8,128)}, u32[]{:S(2)}) copy-start(f32[1,1,512,512]{3,2,1,0:T(8,128)} %param.11) | copy-start | bytes 3145732
  0.7 4.6 %copy-start.11 = (bf16[1,1,128,512]{3,2,1,0:T(8,128)(2,1)S(1)}, bf16[1,1,128,512]{3,2,1,0:T(8,128)(2,1)}, u32[]{:S(2)}) copy-start(bf16[1,1,128,512]{3,2,1,0:T(8,128)(2,1)} %param.9) | copy-start | bytes 393220
  3.2 15.5 %copy-start.4 = (bf16[1,1,512,512]{3,2,1,0:T(8,128)(2,1)S(1)}, bf16[1,1,512,512]{3,2,1,0:T(8,128)(2,1)}, u32[]{:S(2)}) copy-start(bf16[1,1,512,512]{3,2,1,0:T(8,128)(2,1)} %param.10) | copy-start | bytes 1572868
  3.2 15.4 %collective-permute-start = (bf16[1024,512]{1,0:T(8,128)(2,1)S(1)}, bf16[1024,512]{1,0:T(8,128)(2,1)S(1)}, u32[]{:S(2)}, u32[]{:S(2)}) collective-permute-start(bf16[1024,512]{1,0:T(8,128)(2,1)S(1)} %bitcast.53), channel_id=1, source_target_pairs={{0,1},{1,0},{2,3},{3,2},{4,5},{5,4},{6,7},{7,6},{8,9},{9,8},{10,11... | collective-permute-start | bytes 3145736 | tf_op jit(solution)/shard_map/ppermute | solution.py:358
  18.7 1.6 %copy-start.2 = (bf16[1024,512]{1,0:T(8,128)(2,1)}, bf16[1024,512]{1,0:T(8,128)(2,1)S(1)}, u32[]{:S(2)}) copy-start(bf16[1024,512]{1,0:T(8,128)(2,1)S(1)} %collective-permute-done.other_ref) | copy-start | bytes 3145732
  20.2 17.1 %all-to-all-start = ((bf16[4,128,1024]{2,1,0:T(8,128)(2,1)}), bf16[4,128,1024]{2,1,0:T(8,128)(2,1)S(1)}, u32[]{:S(2)}, u32[]{:S(2)}) async-start(bf16[4,128,1024]{2,1,0:T(8,128)(2,1)} %key_back_columns.1), calls=%async_computation | async-start | bytes 2097152 | tf_op jit(solution)/shard_map/all_to_all | solution.py:362
  25.0 2.7 %copy-start.3 = (bf16[1024,512]{1,0:T(8,128)(2,1)S(1)}, bf16[1024,512]{1,0:T(8,128)(2,1)}, u32[]{:S(2)}) copy-start(bf16[1024,512]{1,0:T(8,128)(2,1)} %copy-done.2) | copy-start | bytes 3145732
  25.0 2.7 %copy-start.5 = (bf16[4,128,512]{2,1,0:T(8,128)(2,1)S(1)}, bf16[4,128,512]{2,1,0:T(8,128)(2,1)}, u32[]{:S(2)}) copy-start(bf16[4,128,512]{2,1,0:T(8,128)(2,1)} %get-tuple-element.29.own_ref) | copy-start | bytes 1572868
  25.7 11.6 %copy-start.1 = (bf16[1,1,128,4096]{3,2,1,0:T(8,128)(2,1)S(1)}, bf16[1,1,128,4096]{3,2,1,0:T(8,128)(2,1)}, u32[]{:S(2)}) copy-start(bf16[1,1,128,4096]{3,2,1,0:T(8,128)(2,1)} %param.7) | copy-start | bytes 3145732
  25.7 4.6 %collective-permute-start.1 = (bf16[4,128,256]{2,1,0:T(8,128)(2,1)S(1)}, bf16[4,128,256]{2,1,0:T(8,128)(2,1)S(1)}, u32[]{:S(2)}, u32[]{:S(2)}) collective-permute-start(bf16[4,128,256]{2,1,0:T(8,128)(2,1)S(1)} %convolution_convert_fusion.own_keys), channel_id=1, source_target_pairs={{0,1},{1,0},{2,3},{3,2},{4,5},{5,4},{6,7},{7,6},{8,9},{9,8},{10,11... | collective-permute-start | bytes 786440 | tf_op jit(solution)/shard_map/ppermute | solution.py:371
  27.8 9.5 %copy-start.9 = (f32[1,4096]{1,0:T(1,128)S(1)}, f32[1,4096]{1,0:T(1,128)}, u32[]{:S(2)}) copy-start(f32[1,4096]{1,0:T(1,128)} %gain_ref.3) | copy-start | bytes 49156
  30.3 0.7 copy-start.6
  38.9 8.2 %copy-start.14 = (bf16[2,128,512]{2,1,0:T(8,128)(2,1)S(1)}, bf16[2,128,512]{2,1,0:T(8,128)(2,1)}, u32[]{:S(2)}) copy-start(bf16[2,128,512]{2,1,0:T(8,128)(2,1)} %get-tuple-element.39) | copy-start | bytes 786436
  38.9 10.8 %copy-start.13 = (bf16[2,128,512]{2,1,0:T(8,128)(2,1)S(1)}, bf16[2,128,512]{2,1,0:T(8,128)(2,1)}, u32[]{:S(2)}) copy-start(bf16[2,128,512]{2,1,0:T(8,128)(2,1)} %get-tuple-element.40) | copy-start | bytes 786436
  39.0 14.8 %copy-start.12 = (bf16[2,128,512]{2,1,0:T(8,128)(2,1)S(1)}, bf16[2,128,512]{2,1,0:T(8,128)(2,1)}, u32[]{:S(2)}) copy-start(bf16[2,128,512]{2,1,0:T(8,128)(2,1)} %get-tuple-element.41) | copy-start | bytes 786436
  39.0 34.2 %all-to-all-start.1 = ((bf16[16,8,4096]{2,1,0:T(8,128)(2,1)}), bf16[16,8,4096]{2,1,0:T(8,128)(2,1)S(1)}, u32[]{:S(2)}, u32[]{:S(2)}) async-start(bf16[16,8,4096]{2,1,0:T(8,128)(2,1)} %branch_pieces.1), calls=%async_computation.1 | async-start | bytes 2097152 | tf_op jit(solution)/shard_map/all_to_all | solution.py:377
  47.1 15.3 %copy-start.7 = (bf16[4,128,256]{2,1,0:T(8,128)(2,1)S(1)}, bf16[4,128,256]{2,1,0:T(8,128)(2,1)}, u32[]{:S(2)}) copy-start(bf16[4,128,256]{2,1,0:T(8,128)(2,1)} %copy-done.6) | copy-start | bytes 786436
  47.1 15.3 %copy-start.8 = (bf16[2,128,512]{2,1,0:T(8,128)(2,1)S(1)}, bf16[2,128,512]{2,1,0:T(8,128)(2,1)}, u32[]{:S(2)}) copy-start(bf16[2,128,512]{2,1,0:T(8,128)(2,1)} %get-tuple-element.38.part0) | copy-start | bytes 786436
  47.1 12.8 %collective-permute-start.2 = (bf16[2,128,512]{2,1,0:T(8,128)(2,1)S(1)}, bf16[2,128,512]{2,1,0:T(8,128)(2,1)S(1)}, u32[]{:S(2)}, u32[]{:S(2)}) collective-permute-start(bf16[2,128,512]{2,1,0:T(8,128)(2,1)S(1)} %copy-done.14), channel_id=1, source_target_pairs={{0,2},{1,3},{2,4},{3,5},{4,6},{5,7},{6,0},{7,1},{8,10},{9,11},{10,... | collective-permute-start | bytes 786440 | tf_op jit(solution)/shard_map/ppermute | solution.py:381
  49.8 10.1 %collective-permute-start.3 = (bf16[2,128,512]{2,1,0:T(8,128)(2,1)S(1)}, bf16[2,128,512]{2,1,0:T(8,128)(2,1)S(1)}, u32[]{:S(2)}, u32[]{:S(2)}) collective-permute-start(bf16[2,128,512]{2,1,0:T(8,128)(2,1)S(1)} %copy-done.13), channel_id=1, source_target_pairs={{0,4},{1,5},{2,6},{3,7},{4,0},{5,1},{6,2},{7,3},{8,12},{9,13},{10,... | collective-permute-start | bytes 786440 | tf_op jit(solution)/shard_map/ppermute | solution.py:381
  53.8 8.6 %collective-permute-start.4 = (bf16[2,128,512]{2,1,0:T(8,128)(2,1)S(1)}, bf16[2,128,512]{2,1,0:T(8,128)(2,1)S(1)}, u32[]{:S(2)}, u32[]{:S(2)}) collective-permute-start(bf16[2,128,512]{2,1,0:T(8,128)(2,1)S(1)} %copy-done.12), channel_id=1, source_target_pairs={{0,6},{1,7},{2,0},{3,1},{4,2},{5,3},{6,4},{7,5},{8,14},{9,15},{10,... | collective-permute-start | bytes 786440 | tf_op jit(solution)/shard_map/ppermute | solution.py:381
  63.2 9.9 %collective-permute-start.5 = (bf16[128,512]{1,0:T(8,128)(2,1)S(1)}, bf16[128,512]{1,0:T(8,128)(2,1)S(1)}, u32[]{:S(2)}, u32[]{:S(2)}) collective-permute-start(bf16[128,512]{1,0:T(8,128)(2,1)S(1)} %pad_maximum_fusion), channel_id=1, source_target_pairs={{0,128},{128,0},{256,384},{384,256},{1,129},{129,1},{257,385},{385... | collective-permute-start | bytes 393224 | tf_op jit(solution)/shard_map/ppermute | solution.py:393
  74.3 8.3 %copy-start.10 = (f32[1,64,512]{2,1,0:T(8,128)S(1)}, f32[1,64,512]{2,1,0:T(8,128)}, u32[]{:S(2)}) copy-start(f32[1,64,512]{2,1,0:T(8,128)} %param.12) | copy-start | bytes 393220
  74.3 41.0 %all-to-all-start.2 = ((bf16[16,8,4096]{2,1,0:T(8,128)(2,1)}), bf16[16,8,4096]{2,1,0:T(8,128)(2,1)S(1)}, u32[]{:S(2)}, u32[]{:S(2)}) async-start(bf16[16,8,4096]{2,1,0:T(8,128)(2,1)} %suffix_sums.1), calls=%async_computation.2 | async-start | bytes 2097152 | tf_op jit(solution)/shard_map/all_to_all | solution.py:399

commit v5 on v4

--- a/solution.py
+++ b/solution.py
@@ -395,7 +395,9 @@
     rows = exchange(jnp.concatenate([rows_of(1), rows_of(2)]), 1)
     own_sum = rows_of(0) + rows[:rank_share]
     other_sum = rows_of(3) + rows[rank_share:]
-    sums, own_sum, other_sum = lax.optimization_barrier((suffix_sums(pieces), own_sum, other_sum))
+    sums, own_sum, other_sum, late_basis = lax.optimization_barrier(
+        (suffix_sums(pieces), own_sum, other_sum, basis_row)
+    )
     pieces = lax.all_to_all(sums, "section", 0, 0)
     input_grad = pieces.reshape(tokens, width)
 
@@ -409,7 +411,7 @@
     pair_sums = pair_sums.astype(jnp.float32)
     total = jnp.concatenate([pair_sums[i, 0] + pair_sums[i ^ 3, 1] for i in range(islands)])
     outer_update = (outer_rate * mean_weight) * jnp.einsum(
-        "rd,kr->dk", total, basis_row, precision=lax.Precision.HIGH
+        "rd,kr->dk", total, late_basis, precision=lax.Precision.HIGH
     )
     return (input_grad[None, None], own_momentum[None], outer_update[None])
 

time: 117 us -> 117 us (level)
  transfers between devices with their start and end apart: 9 -> 9, of which waited for: 4 -> 4; matrix products, arithmetic and copies ran while one was open for 4% -> 5% of each run, Pallas kernels for 3% -> 3%
where the time goes in v5:
time: 117 us; the launch traced here: 116 us
  blocking collectives  42.9 us (37%)
  starting transfers between devices  39.8 us (34%)
  waiting for transfers between devices  14.6 us (12%)
  Pallas kernels  9.98 us (9%)
  matrix products  3.93 us (3%)
  local copies, waits for them, and re-layouts  1.77 us (2%)
  between operations  1.69 us (1%)
  other arithmetic  1.34 us (1%)
    all_gather x1, blocking collectives, shards(): pair_sums = lax.all_gather(pair_sums, 'island')  29.5 us
    all_gather x1, blocking collectives, shards(): line_keys = lax.all_gather(sent_keys, 'fsdp', axis_index_groups=x_lines)  13.4 us
    ppermute x3, starting transfers between devices, shards(): parts[turn] = lax.ppermute(parts[turn], 'fsdp', path)  9.11 us
    all_to_all x1, starting transfers between devices, shards(): pieces = lax.all_to_all(sums, 'section', 0, 0)  8.27 us
    all_to_all x1, starting transfers between devices, shards(): pieces = lax.all_to_all(pieces, 'section', 0, 0)  8.16 us
    all_to_all x1, waiting for transfers between devices, shards(): back = lax.all_to_all(back, 'fsdp', 0, 0, axis_index_groups=x_lines)  6.3 us
    ppermute x1, starting transfers between devices, exchange(): lax.ppermute(rows.astype(jnp.bfloat16), 'island', path).astype(jnp.float32)  6.04 us
    ppermute x3, waiting for transfers between devices, shards(): parts[turn] = lax.ppermute(parts[turn], 'fsdp', path)  4.8 us
  transfers between devices with their start and end apart: 9, of which 4 were waited for; matrix products, arithmetic and copies ran while one was open for 5% of the time, Pallas kernels for 3%

profile of v5, /device:TPU:104, one launch (start us, length us, event | category | flops | bytes accessed | tf_op | source)
XLA Modules:
  0.0 116.0 jit_solution(3843513693933291458)
XLA Ops:
  0.7 2.5 %prepare.1 = (bf16[4,128,512]{2,1,0:T(8,128)(2,1)}, bf16[8,128,512]{2,1,0:T(8,128)(2,1)S(1)}) custom-call(s32[1]{0:T(128)} %bitcast.1.core_ref, bf16[128,4096]{1,0:T(8,128)(2,1)} %bitcast.48, f32[1,4096]{1,0:T(1,128)} %gain_ref.3, bf16[4,128,512]{2,1,0:T(8,128)(2,1)} %bitcast.52), custom_call_target="tpu_custom_call" | custom-call | tf_op jit(solution)/shard_map/prepare/pallas_call | solution.py:192
  3.2 2.1 %collective-permute-start = (bf16[1024,512]{1,0:T(8,128)(2,1)S(1)}, bf16[1024,512]{1,0:T(8,128)(2,1)S(1)}, u32[]{:S(2)}, u32[]{:S(2)}) collective-permute-start(bf16[1024,512]{1,0:T(8,128)(2,1)S(1)} %bitcast.54), channel_id=1, source_target_pairs={{0,1},{1,0},{2,3},{3,2},{4,5},{5,4},{6,7},{7,6},{8,9},{9,8},{10,11... | collective-permute-start | bytes 3145736 | tf_op jit(solution)/shard_map/ppermute | solution.py:358
  5.3 13.4 %all-gather = bf16[512,512]{1,0:T(8,128)(2,1)S(1)} all-gather(bf16[128,512]{1,0:T(8,128)(2,1)S(1)} %bitcast.57), channel_id=2, replica_groups={{0,2,4,6},{1,3,5,7},{8,10,12,14},{9,11,13,15},{16,18,20,22},{17,19,21,2..., dimensions={0}, use_global_device_ids=true | all-gather | bytes 655360 | tf_op jit(solution)/shard_map/all_gather | solution.py:359
  18.7 1.5 %key_back_columns.1 = bf16[4,128,1024]{2,1,0:T(8,128)(2,1)} custom-call(s32[1]{0:T(128)} %bitcast.1.core_ref, bf16[4,128,512]{2,1,0:T(8,128)(2,1)S(1)} %bitcast.50, bf16[512,512]{1,0:T(8,128)(2,1)S(1)} %bitcast.53, bf16[1024,512]{1,0:T(8,128)(2,1)S(1)} %collective-permute-done.other_ref), custom_call_target="tpu_custom_call" | custom-call | tf_op jit(solution)/shard_map/key_back_columns/pallas_call | solution.py:122
  20.2 4.1 %all-to-all-start = ((bf16[4,128,1024]{2,1,0:T(8,128)(2,1)}), bf16[4,128,1024]{2,1,0:T(8,128)(2,1)S(1)}, u32[]{:S(2)}, u32[]{:S(2)}) async-start(bf16[4,128,1024]{2,1,0:T(8,128)(2,1)} %key_back_columns.1), calls=%async_computation | async-start | bytes 2097152 | tf_op jit(solution)/shard_map/all_to_all | solution.py:362
  25.7 2.1 %collective-permute-start.1 = (bf16[4,128,256]{2,1,0:T(8,128)(2,1)S(1)}, bf16[4,128,256]{2,1,0:T(8,128)(2,1)S(1)}, u32[]{:S(2)}, u32[]{:S(2)}) collective-permute-start(bf16[4,128,256]{2,1,0:T(8,128)(2,1)S(1)} %convolution_convert_fusion.own_keys), channel_id=1, source_target_pairs={{0,1},{1,0},{2,3},{3,2},{4,5},{5,4},{6,7},{7,6},{8,9},{9,8},{10,11... | collective-permute-start | bytes 786440 | tf_op jit(solution)/shard_map/ppermute | solution.py:371
  27.8 2.5 %pair_columns.1 = (bf16[2,128,512]{2,1,0:T(8,128)(2,1)}, bf16[2,128,512]{2,1,0:T(8,128)(2,1)}, bf16[2,128,512]{2,1,0:T(8,128)(2,1)}, bf16[2,128,512]{2,1,0:T(8,128)(2,1)}) custom-call(s32[1]{0:T(128)} %bitcast.9.chip_ref, bf16[4,128,512]{2,1,0:T(8,128)(2,1)S(1)} %copy-done.5, bf16[1024,512]{1,0:T(8,128)(2,1)S(1)} %copy-done.3), custom_call_target="tpu_custom_call" | custom-call | tf_op jit(solution)/shard_map/pair_columns/pallas_call | solution.py:244
  31.0 6.3 %all-to-all-done.back_ref = bf16[4,128,1024]{2,1,0:T(8,128)(2,1)S(1)} async-done(((bf16[4,128,1024]{2,1,0:T(8,128)(2,1)}), bf16[4,128,1024]{2,1,0:T(8,128)(2,1)S(1)}, u32[]{:S(2)}, u32[]{:S(2)}) %all-to-all-start) | async-done | bytes 1048608 | tf_op jit(solution)/shard_map/all_to_all | solution.py:362
  37.3 1.6 %branch_pieces.1 = bf16[16,8,4096]{2,1,0:T(8,128)(2,1)} custom-call(bf16[128,4096]{1,0:T(8,128)(2,1)S(1)} %bitcast.49, bf16[4,128,1024]{2,1,0:T(8,128)(2,1)S(1)} %all-to-all-done.back_ref, f32[1,4096]{1,0:T(1,128)S(1)} %copy-done.9), custom_call_target="tpu_custom_call" | custom-call | tf_op jit(solution)/shard_map/branch_pieces/pallas_call | solution.py:329
  39.0 8.2 %all-to-all-start.1 = ((bf16[16,8,4096]{2,1,0:T(8,128)(2,1)}), bf16[16,8,4096]{2,1,0:T(8,128)(2,1)S(1)}, u32[]{:S(2)}, u32[]{:S(2)}) async-start(bf16[16,8,4096]{2,1,0:T(8,128)(2,1)} %branch_pieces.1), calls=%async_computation.1 | async-start | bytes 2097152 | tf_op jit(solution)/shard_map/all_to_all | solution.py:377
  47.1 2.6 %collective-permute-start.2 = (bf16[2,128,512]{2,1,0:T(8,128)(2,1)S(1)}, bf16[2,128,512]{2,1,0:T(8,128)(2,1)S(1)}, u32[]{:S(2)}, u32[]{:S(2)}) collective-permute-start(bf16[2,128,512]{2,1,0:T(8,128)(2,1)S(1)} %copy-done.14), channel_id=1, source_target_pairs={{0,2},{1,3},{2,4},{3,5},{4,6},{5,7},{6,0},{7,1},{8,10},{9,11},{10,... | collective-permute-start | bytes 786440 | tf_op jit(solution)/shard_map/ppermute | solution.py:381
  49.8 4.0 %collective-permute-start.3 = (bf16[2,128,512]{2,1,0:T(8,128)(2,1)S(1)}, bf16[2,128,512]{2,1,0:T(8,128)(2,1)S(1)}, u32[]{:S(2)}, u32[]{:S(2)}) collective-permute-start(bf16[2,128,512]{2,1,0:T(8,128)(2,1)S(1)} %copy-done.13), channel_id=1, source_target_pairs={{0,4},{1,5},{2,6},{3,7},{4,0},{5,1},{6,2},{7,3},{8,12},{9,13},{10,... | collective-permute-start | bytes 786440 | tf_op jit(solution)/shard_map/ppermute | solution.py:381
  53.8 2.5 %collective-permute-start.4 = (bf16[2,128,512]{2,1,0:T(8,128)(2,1)S(1)}, bf16[2,128,512]{2,1,0:T(8,128)(2,1)S(1)}, u32[]{:S(2)}, u32[]{:S(2)}) collective-permute-start(bf16[2,128,512]{2,1,0:T(8,128)(2,1)S(1)} %copy-done.12), channel_id=1, source_target_pairs={{0,6},{1,7},{2,0},{3,1},{4,2},{5,3},{6,4},{7,5},{8,14},{9,15},{10,... | collective-permute-start | bytes 786440 | tf_op jit(solution)/shard_map/ppermute | solution.py:381
  56.3 1.3 %fusion.1.drift_ref = f32[256,512]{1,0:T(8,128)S(1)} fusion(f32[1,1,512,512]{3,2,1,0:T(8,128)S(1)} %copy-done, s32[]{:T(128)} %bitcast.7, s32[512]{0:T(512)S(1)} %iota_multiply_fusion), kind=kOutput, calls=%fused_computation.3 | convolution fusion | flops 404750336 | bytes 1574916 | tf_op jit(solution)/shard_map/kr,dk->rd/dot_general | solution.py:382
  57.6 2.3 %collective-permute-done.2.part1 = bf16[2,128,512]{2,1,0:T(8,128)(2,1)S(1)} collective-permute-done((bf16[2,128,512]{2,1,0:T(8,128)(2,1)S(1)}, bf16[2,128,512]{2,1,0:T(8,128)(2,1)S(1)}, u32[]{:S(2)}, u32[]{:S(2)}) %collective-permute-start.2) | collective-permute-done | bytes 262176 | tf_op jit(solution)/shard_map/ppermute | solution.py:381
  59.9 2.5 %collective-permute-done.4.part3 = bf16[2,128,512]{2,1,0:T(8,128)(2,1)S(1)} collective-permute-done((bf16[2,128,512]{2,1,0:T(8,128)(2,1)S(1)}, bf16[2,128,512]{2,1,0:T(8,128)(2,1)S(1)}, u32[]{:S(2)}, u32[]{:S(2)}) %collective-permute-start.4) | collective-permute-done | bytes 262176 | tf_op jit(solution)/shard_map/ppermute | solution.py:381
  62.4 0.7 factor_columns.1
  63.2 6.0 %collective-permute-start.5 = (bf16[128,512]{1,0:T(8,128)(2,1)S(1)}, bf16[128,512]{1,0:T(8,128)(2,1)S(1)}, u32[]{:S(2)}, u32[]{:S(2)}) collective-permute-start(bf16[128,512]{1,0:T(8,128)(2,1)S(1)} %pad_maximum_fusion), channel_id=1, source_target_pairs={{0,128},{128,0},{256,384},{384,256},{1,129},{129,1},{257,385},{385... | collective-permute-start | bytes 393224 | tf_op jit(solution)/shard_map/ppermute | solution.py:393
  69.6 3.5 %collective-permute-done.5 = bf16[128,512]{1,0:T(8,128)(2,1)S(1)} collective-permute-done((bf16[128,512]{1,0:T(8,128)(2,1)S(1)}, bf16[128,512]{1,0:T(8,128)(2,1)S(1)}, u32[]{:S(2)}, u32[]{:S(2)}) %collective-permute-start.5) | collective-permute-done | bytes 131104 | tf_op jit(solution)/shard_map/ppermute | solution.py:393
  73.2 1.0 suffix_sums.1
  74.3 8.3 %all-to-all-start.2 = ((bf16[16,8,4096]{2,1,0:T(8,128)(2,1)}), bf16[16,8,4096]{2,1,0:T(8,128)(2,1)S(1)}, u32[]{:S(2)}, u32[]{:S(2)}) async-start(bf16[16,8,4096]{2,1,0:T(8,128)(2,1)} %suffix_sums.1), calls=%async_computation.2 | async-start | bytes 2097152 | tf_op jit(solution)/shard_map/all_to_all | solution.py:401
  82.6 29.5 %all_gather.12 = bf16[4,2,64,512]{3,2,1,0:T(8,128)(2,1)S(1)} all-gather(bf16[1,2,64,512]{3,2,1,0:T(8,128)(2,1)S(1)} %pad_maximum_fusion.1), channel_id=1, replica_groups=mesh['island'=4,'section'=16,'fsdp'=8] {'island'}, dimensions={0}, use_global_device_ids=true | all-gather | bytes 655360 | tf_op jit(solution)/shard_map/all_gather | solution.py:407
  112.3 2.0 %fusion = f32[1,512,512]{2,1,0:T(8,128)} fusion(f32[512,256]{1,0:T(8,128)S(1)} %fusion.9, f32[64,512]{1,0:T(8,128)S(1)} %get-tuple-element.50, f32[64,512]{1,0:T(8,128)S(1)} %get-tuple-element.49, f32[64,512]{1,0:T(8,128)S(1)} %get-tuple-element.48, f32[64,512]{1,0:T(8,128)S(1)} %get-tuple-element.47), kind=kOutput, calls=%fused_computation.1 | convolution fusion | flops 403308544 | bytes 2097152 | tf_op jit(solution)/shard_map/rd,kr->dk/dot_general | solution.py:413
  115.0 1.0 copy.12
  (48 shorter events, 2.8 us)
Async XLA Ops:
  0.6 55.7 %copy-start = (f32[1,1,512,512]{3,2,1,0:T(8,128)S(1)}, f32[1,1,512,512]{3,2,1,0:T(8,128)}, u32[]{:S(2)}) copy-start(f32[1,1,512,512]{3,2,1,0:T(8,128)} %param.11) | copy-start | bytes 3145732
  0.7 4.6 %copy-start.11 = (bf16[1,1,128,512]{3,2,1,0:T(8,128)(2,1)S(1)}, bf16[1,1,128,512]{3,2,1,0:T(8,128)(2,1)}, u32[]{:S(2)}) copy-start(bf16[1,1,128,512]{3,2,1,0:T(8,128)(2,1)} %param.9) | copy-start | bytes 393220
  3.2 15.5 %copy-start.4 = (bf16[1,1,512,512]{3,2,1,0:T(8,128)(2,1)S(1)}, bf16[1,1,512,512]{3,2,1,0:T(8,128)(2,1)}, u32[]{:S(2)}) copy-start(bf16[1,1,512,512]{3,2,1,0:T(8,128)(2,1)} %param.10) | copy-start | bytes 1572868
  3.2 15.4 %collective-permute-start = (bf16[1024,512]{1,0:T(8,128)(2,1)S(1)}, bf16[1024,512]{1,0:T(8,128)(2,1)S(1)}, u32[]{:S(2)}, u32[]{:S(2)}) collective-permute-start(bf16[1024,512]{1,0:T(8,128)(2,1)S(1)} %bitcast.54), channel_id=1, source_target_pairs={{0,1},{1,0},{2,3},{3,2},{4,5},{5,4},{6,7},{7,6},{8,9},{9,8},{10,11... | collective-permute-start | bytes 3145736 | tf_op jit(solution)/shard_map/ppermute | solution.py:358
  18.7 1.6 %copy-start.2 = (bf16[1024,512]{1,0:T(8,128)(2,1)}, bf16[1024,512]{1,0:T(8,128)(2,1)S(1)}, u32[]{:S(2)}) copy-start(bf16[1024,512]{1,0:T(8,128)(2,1)S(1)} %collective-permute-done.other_ref) | copy-start | bytes 3145732
  20.2 17.1 %all-to-all-start = ((bf16[4,128,1024]{2,1,0:T(8,128)(2,1)}), bf16[4,128,1024]{2,1,0:T(8,128)(2,1)S(1)}, u32[]{:S(2)}, u32[]{:S(2)}) async-start(bf16[4,128,1024]{2,1,0:T(8,128)(2,1)} %key_back_columns.1), calls=%async_computation | async-start | bytes 2097152 | tf_op jit(solution)/shard_map/all_to_all | solution.py:362
  25.0 2.7 %copy-start.3 = (bf16[1024,512]{1,0:T(8,128)(2,1)S(1)}, bf16[1024,512]{1,0:T(8,128)(2,1)}, u32[]{:S(2)}) copy-start(bf16[1024,512]{1,0:T(8,128)(2,1)} %copy-done.2) | copy-start | bytes 3145732
  25.0 2.7 %copy-start.5 = (bf16[4,128,512]{2,1,0:T(8,128)(2,1)S(1)}, bf16[4,128,512]{2,1,0:T(8,128)(2,1)}, u32[]{:S(2)}) copy-start(bf16[4,128,512]{2,1,0:T(8,128)(2,1)} %get-tuple-element.30.own_ref) | copy-start | bytes 1572868
  25.7 11.6 %copy-start.1 = (bf16[1,1,128,4096]{3,2,1,0:T(8,128)(2,1)S(1)}, bf16[1,1,128,4096]{3,2,1,0:T(8,128)(2,1)}, u32[]{:S(2)}) copy-start(bf16[1,1,128,4096]{3,2,1,0:T(8,128)(2,1)} %param.7) | copy-start | bytes 3145732
  25.7 4.6 %collective-permute-start.1 = (bf16[4,128,256]{2,1,0:T(8,128)(2,1)S(1)}, bf16[4,128,256]{2,1,0:T(8,128)(2,1)S(1)}, u32[]{:S(2)}, u32[]{:S(2)}) collective-permute-start(bf16[4,128,256]{2,1,0:T(8,128)(2,1)S(1)} %convolution_convert_fusion.own_keys), channel_id=1, source_target_pairs={{0,1},{1,0},{2,3},{3,2},{4,5},{5,4},{6,7},{7,6},{8,9},{9,8},{10,11... | collective-permute-start | bytes 786440 | tf_op jit(solution)/shard_map/ppermute | solution.py:371
  27.8 9.5 %copy-start.9 = (f32[1,4096]{1,0:T(1,128)S(1)}, f32[1,4096]{1,0:T(1,128)}, u32[]{:S(2)}) copy-start(f32[1,4096]{1,0:T(1,128)} %gain_ref.3) | copy-start | bytes 49156
  30.3 0.7 copy-start.6
  38.9 8.2 %copy-start.14 = (bf16[2,128,512]{2,1,0:T(8,128)(2,1)S(1)}, bf16[2,128,512]{2,1,0:T(8,128)(2,1)}, u32[]{:S(2)}) copy-start(bf16[2,128,512]{2,1,0:T(8,128)(2,1)} %get-tuple-element.40) | copy-start | bytes 786436
  38.9 10.8 %copy-start.13 = (bf16[2,128,512]{2,1,0:T(8,128)(2,1)S(1)}, bf16[2,128,512]{2,1,0:T(8,128)(2,1)}, u32[]{:S(2)}) copy-start(bf16[2,128,512]{2,1,0:T(8,128)(2,1)} %get-tuple-element.41) | copy-start | bytes 786436
  39.0 14.8 %copy-start.12 = (bf16[2,128,512]{2,1,0:T(8,128)(2,1)S(1)}, bf16[2,128,512]{2,1,0:T(8,128)(2,1)}, u32[]{:S(2)}) copy-start(bf16[2,128,512]{2,1,0:T(8,128)(2,1)} %get-tuple-element.42) | copy-start | bytes 786436
  39.0 34.2 %all-to-all-start.1 = ((bf16[16,8,4096]{2,1,0:T(8,128)(2,1)}), bf16[16,8,4096]{2,1,0:T(8,128)(2,1)S(1)}, u32[]{:S(2)}, u32[]{:S(2)}) async-start(bf16[16,8,4096]{2,1,0:T(8,128)(2,1)} %branch_pieces.1), calls=%async_computation.1 | async-start | bytes 2097152 | tf_op jit(solution)/shard_map/all_to_all | solution.py:377
  47.1 15.3 %copy-start.7 = (bf16[4,128,256]{2,1,0:T(8,128)(2,1)S(1)}, bf16[4,128,256]{2,1,0:T(8,128)(2,1)}, u32[]{:S(2)}) copy-start(bf16[4,128,256]{2,1,0:T(8,128)(2,1)} %copy-done.6) | copy-start | bytes 786436
  47.1 15.3 %copy-start.8 = (bf16[2,128,512]{2,1,0:T(8,128)(2,1)S(1)}, bf16[2,128,512]{2,1,0:T(8,128)(2,1)}, u32[]{:S(2)}) copy-start(bf16[2,128,512]{2,1,0:T(8,128)(2,1)} %get-tuple-element.39.part0) | copy-start | bytes 786436
  47.1 12.8 %collective-permute-start.2 = (bf16[2,128,512]{2,1,0:T(8,128)(2,1)S(1)}, bf16[2,128,512]{2,1,0:T(8,128)(2,1)S(1)}, u32[]{:S(2)}, u32[]{:S(2)}) collective-permute-start(bf16[2,128,512]{2,1,0:T(8,128)(2,1)S(1)} %copy-done.14), channel_id=1, source_target_pairs={{0,2},{1,3},{2,4},{3,5},{4,6},{5,7},{6,0},{7,1},{8,10},{9,11},{10,... | collective-permute-start | bytes 786440 | tf_op jit(solution)/shard_map/ppermute | solution.py:381
  49.8 10.1 %collective-permute-start.3 = (bf16[2,128,512]{2,1,0:T(8,128)(2,1)S(1)}, bf16[2,128,512]{2,1,0:T(8,128)(2,1)S(1)}, u32[]{:S(2)}, u32[]{:S(2)}) collective-permute-start(bf16[2,128,512]{2,1,0:T(8,128)(2,1)S(1)} %copy-done.13), channel_id=1, source_target_pairs={{0,4},{1,5},{2,6},{3,7},{4,0},{5,1},{6,2},{7,3},{8,12},{9,13},{10,... | collective-permute-start | bytes 786440 | tf_op jit(solution)/shard_map/ppermute | solution.py:381
  53.8 8.6 %collective-permute-start.4 = (bf16[2,128,512]{2,1,0:T(8,128)(2,1)S(1)}, bf16[2,128,512]{2,1,0:T(8,128)(2,1)S(1)}, u32[]{:S(2)}, u32[]{:S(2)}) collective-permute-start(bf16[2,128,512]{2,1,0:T(8,128)(2,1)S(1)} %copy-done.12), channel_id=1, source_target_pairs={{0,6},{1,7},{2,0},{3,1},{4,2},{5,3},{6,4},{7,5},{8,14},{9,15},{10,... | collective-permute-start | bytes 786440 | tf_op jit(solution)/shard_map/ppermute | solution.py:381
  63.2 9.9 %collective-permute-start.5 = (bf16[128,512]{1,0:T(8,128)(2,1)S(1)}, bf16[128,512]{1,0:T(8,128)(2,1)S(1)}, u32[]{:S(2)}, u32[]{:S(2)}) collective-permute-start(bf16[128,512]{1,0:T(8,128)(2,1)S(1)} %pad_maximum_fusion), channel_id=1, source_target_pairs={{0,128},{128,0},{256,384},{384,256},{1,129},{129,1},{257,385},{385... | collective-permute-start | bytes 393224 | tf_op jit(solution)/shard_map/ppermute | solution.py:393
  74.3 8.3 %copy-start.10 = (f32[1,64,512]{2,1,0:T(8,128)S(1)}, f32[1,64,512]{2,1,0:T(8,128)}, u32[]{:S(2)}) copy-start(f32[1,64,512]{2,1,0:T(8,128)} %param.12) | copy-start | bytes 393220
  74.3 40.8 %all-to-all-start.2 = ((bf16[16,8,4096]{2,1,0:T(8,128)(2,1)}), bf16[16,8,4096]{2,1,0:T(8,128)(2,1)S(1)}, u32[]{:S(2)}, u32[]{:S(2)}) async-start(bf16[16,8,4096]{2,1,0:T(8,128)(2,1)} %suffix_sums.1), calls=%async_computation.2 | async-start | bytes 2097152 | tf_op jit(solution)/shard_map/all_to_all | solution.py:401

commit v6 on v5

--- a/solution.py
+++ b/solution.py
@@ -73,7 +73,7 @@
 
 def suffix_sums(parts):
     count, rows, width = parts.shape
-    step = 512
+    step = 1024
     chunks = width // step
     return pl.pallas_call(
         suffix_kernel,

time: 117 us -> 117 us (level)
  no operation moved by 1% of the time
where the time goes in v6:
time: 117 us; the launch traced here: 116 us
  blocking collectives  42.9 us (37%)
  starting transfers between devices  39.8 us (34%)
  waiting for transfers between devices  14.6 us (12%)
  Pallas kernels  9.97 us (9%)
  matrix products  3.93 us (3%)
  local copies, waits for them, and re-layouts  1.77 us (2%)
  between operations  1.69 us (1%)
  other arithmetic  1.34 us (1%)
    all_gather x1, blocking collectives, shards(): pair_sums = lax.all_gather(pair_sums, 'island')  29.5 us
    all_gather x1, blocking collectives, shards(): line_keys = lax.all_gather(sent_keys, 'fsdp', axis_index_groups=x_lines)  13.4 us
    ppermute x3, starting transfers between devices, shards(): parts[turn] = lax.ppermute(parts[turn], 'fsdp', path)  9.11 us
    all_to_all x1, starting transfers between devices, shards(): pieces = lax.all_to_all(sums, 'section', 0, 0)  8.27 us
    all_to_all x1, starting transfers between devices, shards(): pieces = lax.all_to_all(pieces, 'section', 0, 0)  8.16 us
    all_to_all x1, waiting for transfers between devices, shards(): back = lax.all_to_all(back, 'fsdp', 0, 0, axis_index_groups=x_lines)  6.3 us
    ppermute x1, starting transfers between devices, exchange(): lax.ppermute(rows.astype(jnp.bfloat16), 'island', path).astype(jnp.float32)  6.04 us
    ppermute x3, waiting for transfers between devices, shards(): parts[turn] = lax.ppermute(parts[turn], 'fsdp', path)  4.8 us
  transfers between devices with their start and end apart: 9, of which 4 were waited for; matrix products, arithmetic and copies ran while one was open for 5% of the time, Pallas kernels for 3%

profile of v6, /device:TPU:104, one launch (start us, length us, event | category | flops | bytes accessed | tf_op | source)
XLA Modules:
  0.0 116.0 jit_solution(10616531687869837032)
XLA Ops:
  0.7 2.5 %prepare.1 = (bf16[4,128,512]{2,1,0:T(8,128)(2,1)}, bf16[8,128,512]{2,1,0:T(8,128)(2,1)S(1)}) custom-call(s32[1]{0:T(128)} %bitcast.1.core_ref, bf16[128,4096]{1,0:T(8,128)(2,1)} %bitcast.48, f32[1,4096]{1,0:T(1,128)} %gain_ref.3, bf16[4,128,512]{2,1,0:T(8,128)(2,1)} %bitcast.52), custom_call_target="tpu_custom_call" | custom-call | tf_op jit(solution)/shard_map/prepare/pallas_call | solution.py:192
  3.2 2.1 %collective-permute-start = (bf16[1024,512]{1,0:T(8,128)(2,1)S(1)}, bf16[1024,512]{1,0:T(8,128)(2,1)S(1)}, u32[]{:S(2)}, u32[]{:S(2)}) collective-permute-start(bf16[1024,512]{1,0:T(8,128)(2,1)S(1)} %bitcast.54), channel_id=1, source_target_pairs={{0,1},{1,0},{2,3},{3,2},{4,5},{5,4},{6,7},{7,6},{8,9},{9,8},{10,11... | collective-permute-start | bytes 3145736 | tf_op jit(solution)/shard_map/ppermute | solution.py:358
  5.3 13.4 %all-gather = bf16[512,512]{1,0:T(8,128)(2,1)S(1)} all-gather(bf16[128,512]{1,0:T(8,128)(2,1)S(1)} %bitcast.57), channel_id=2, replica_groups={{0,2,4,6},{1,3,5,7},{8,10,12,14},{9,11,13,15},{16,18,20,22},{17,19,21,2..., dimensions={0}, use_global_device_ids=true | all-gather | bytes 655360 | tf_op jit(solution)/shard_map/all_gather | solution.py:359
  18.7 1.5 %key_back_columns.1 = bf16[4,128,1024]{2,1,0:T(8,128)(2,1)} custom-call(s32[1]{0:T(128)} %bitcast.1.core_ref, bf16[4,128,512]{2,1,0:T(8,128)(2,1)S(1)} %bitcast.50, bf16[512,512]{1,0:T(8,128)(2,1)S(1)} %bitcast.53, bf16[1024,512]{1,0:T(8,128)(2,1)S(1)} %collective-permute-done.other_ref), custom_call_target="tpu_custom_call" | custom-call | tf_op jit(solution)/shard_map/key_back_columns/pallas_call | solution.py:122
  20.2 4.1 %all-to-all-start = ((bf16[4,128,1024]{2,1,0:T(8,128)(2,1)}), bf16[4,128,1024]{2,1,0:T(8,128)(2,1)S(1)}, u32[]{:S(2)}, u32[]{:S(2)}) async-start(bf16[4,128,1024]{2,1,0:T(8,128)(2,1)} %key_back_columns.1), calls=%async_computation | async-start | bytes 2097152 | tf_op jit(solution)/shard_map/all_to_all | solution.py:362
  25.7 2.1 %collective-permute-start.1 = (bf16[4,128,256]{2,1,0:T(8,128)(2,1)S(1)}, bf16[4,128,256]{2,1,0:T(8,128)(2,1)S(1)}, u32[]{:S(2)}, u32[]{:S(2)}) collective-permute-start(bf16[4,128,256]{2,1,0:T(8,128)(2,1)S(1)} %convolution_convert_fusion.own_keys), channel_id=1, source_target_pairs={{0,1},{1,0},{2,3},{3,2},{4,5},{5,4},{6,7},{7,6},{8,9},{9,8},{10,11... | collective-permute-start | bytes 786440 | tf_op jit(solution)/shard_map/ppermute | solution.py:371
  27.8 2.5 %pair_columns.1 = (bf16[2,128,512]{2,1,0:T(8,128)(2,1)}, bf16[2,128,512]{2,1,0:T(8,128)(2,1)}, bf16[2,128,512]{2,1,0:T(8,128)(2,1)}, bf16[2,128,512]{2,1,0:T(8,128)(2,1)}) custom-call(s32[1]{0:T(128)} %bitcast.9.chip_ref, bf16[4,128,512]{2,1,0:T(8,128)(2,1)S(1)} %copy-done.5, bf16[1024,512]{1,0:T(8,128)(2,1)S(1)} %copy-done.3), custom_call_target="tpu_custom_call" | custom-call | tf_op jit(solution)/shard_map/pair_columns/pallas_call | solution.py:244
  31.0 6.3 %all-to-all-done.back_ref = bf16[4,128,1024]{2,1,0:T(8,128)(2,1)S(1)} async-done(((bf16[4,128,1024]{2,1,0:T(8,128)(2,1)}), bf16[4,128,1024]{2,1,0:T(8,128)(2,1)S(1)}, u32[]{:S(2)}, u32[]{:S(2)}) %all-to-all-start) | async-done | bytes 1048608 | tf_op jit(solution)/shard_map/all_to_all | solution.py:362
  37.3 1.6 %branch_pieces.1 = bf16[16,8,4096]{2,1,0:T(8,128)(2,1)} custom-call(bf16[128,4096]{1,0:T(8,128)(2,1)S(1)} %bitcast.49, bf16[4,128,1024]{2,1,0:T(8,128)(2,1)S(1)} %all-to-all-done.back_ref, f32[1,4096]{1,0:T(1,128)S(1)} %copy-done.9), custom_call_target="tpu_custom_call" | custom-call | tf_op jit(solution)/shard_map/branch_pieces/pallas_call | solution.py:329
  39.0 8.2 %all-to-all-start.1 = ((bf16[16,8,4096]{2,1,0:T(8,128)(2,1)}), bf16[16,8,4096]{2,1,0:T(8,128)(2,1)S(1)}, u32[]{:S(2)}, u32[]{:S(2)}) async-start(bf16[16,8,4096]{2,1,0:T(8,128)(2,1)} %branch_pieces.1), calls=%async_computation.1 | async-start | bytes 2097152 | tf_op jit(solution)/shard_map/all_to_all | solution.py:377
  47.1 2.6 %collective-permute-start.2 = (bf16[2,128,512]{2,1,0:T(8,128)(2,1)S(1)}, bf16[2,128,512]{2,1,0:T(8,128)(2,1)S(1)}, u32[]{:S(2)}, u32[]{:S(2)}) collective-permute-start(bf16[2,128,512]{2,1,0:T(8,128)(2,1)S(1)} %copy-done.14), channel_id=1, source_target_pairs={{0,2},{1,3},{2,4},{3,5},{4,6},{5,7},{6,0},{7,1},{8,10},{9,11},{10,... | collective-permute-start | bytes 786440 | tf_op jit(solution)/shard_map/ppermute | solution.py:381
  49.8 4.0 %collective-permute-start.3 = (bf16[2,128,512]{2,1,0:T(8,128)(2,1)S(1)}, bf16[2,128,512]{2,1,0:T(8,128)(2,1)S(1)}, u32[]{:S(2)}, u32[]{:S(2)}) collective-permute-start(bf16[2,128,512]{2,1,0:T(8,128)(2,1)S(1)} %copy-done.13), channel_id=1, source_target_pairs={{0,4},{1,5},{2,6},{3,7},{4,0},{5,1},{6,2},{7,3},{8,12},{9,13},{10,... | collective-permute-start | bytes 786440 | tf_op jit(solution)/shard_map/ppermute | solution.py:381
  53.8 2.5 %collective-permute-start.4 = (bf16[2,128,512]{2,1,0:T(8,128)(2,1)S(1)}, bf16[2,128,512]{2,1,0:T(8,128)(2,1)S(1)}, u32[]{:S(2)}, u32[]{:S(2)}) collective-permute-start(bf16[2,128,512]{2,1,0:T(8,128)(2,1)S(1)} %copy-done.12), channel_id=1, source_target_pairs={{0,6},{1,7},{2,0},{3,1},{4,2},{5,3},{6,4},{7,5},{8,14},{9,15},{10,... | collective-permute-start | bytes 786440 | tf_op jit(solution)/shard_map/ppermute | solution.py:381
  56.3 1.3 %fusion.1.drift_ref = f32[256,512]{1,0:T(8,128)S(1)} fusion(f32[1,1,512,512]{3,2,1,0:T(8,128)S(1)} %copy-done, s32[]{:T(128)} %bitcast.7, s32[512]{0:T(512)S(1)} %iota_multiply_fusion), kind=kOutput, calls=%fused_computation.3 | convolution fusion | flops 404750336 | bytes 1574916 | tf_op jit(solution)/shard_map/kr,dk->rd/dot_general | solution.py:382
  57.6 2.3 %collective-permute-done.2.part1 = bf16[2,128,512]{2,1,0:T(8,128)(2,1)S(1)} collective-permute-done((bf16[2,128,512]{2,1,0:T(8,128)(2,1)S(1)}, bf16[2,128,512]{2,1,0:T(8,128)(2,1)S(1)}, u32[]{:S(2)}, u32[]{:S(2)}) %collective-permute-start.2) | collective-permute-done | bytes 262176 | tf_op jit(solution)/shard_map/ppermute | solution.py:381
  59.9 2.5 %collective-permute-done.4.part3 = bf16[2,128,512]{2,1,0:T(8,128)(2,1)S(1)} collective-permute-done((bf16[2,128,512]{2,1,0:T(8,128)(2,1)S(1)}, bf16[2,128,512]{2,1,0:T(8,128)(2,1)S(1)}, u32[]{:S(2)}, u32[]{:S(2)}) %collective-permute-start.4) | collective-permute-done | bytes 262176 | tf_op jit(solution)/shard_map/ppermute | solution.py:381
  62.4 0.7 factor_columns.1
  63.2 6.0 %collective-permute-start.5 = (bf16[128,512]{1,0:T(8,128)(2,1)S(1)}, bf16[128,512]{1,0:T(8,128)(2,1)S(1)}, u32[]{:S(2)}, u32[]{:S(2)}) collective-permute-start(bf16[128,512]{1,0:T(8,128)(2,1)S(1)} %pad_maximum_fusion), channel_id=1, source_target_pairs={{0,128},{128,0},{256,384},{384,256},{1,129},{129,1},{257,385},{385... | collective-permute-start | bytes 393224 | tf_op jit(solution)/shard_map/ppermute | solution.py:393
  69.6 3.5 %collective-permute-done.5 = bf16[128,512]{1,0:T(8,128)(2,1)S(1)} collective-permute-done((bf16[128,512]{1,0:T(8,128)(2,1)S(1)}, bf16[128,512]{1,0:T(8,128)(2,1)S(1)}, u32[]{:S(2)}, u32[]{:S(2)}) %collective-permute-start.5) | collective-permute-done | bytes 131104 | tf_op jit(solution)/shard_map/ppermute | solution.py:393
  73.2 1.0 suffix_sums.1
  74.3 8.3 %all-to-all-start.2 = ((bf16[16,8,4096]{2,1,0:T(8,128)(2,1)}), bf16[16,8,4096]{2,1,0:T(8,128)(2,1)S(1)}, u32[]{:S(2)}, u32[]{:S(2)}) async-start(bf16[16,8,4096]{2,1,0:T(8,128)(2,1)} %suffix_sums.1), calls=%async_computation.2 | async-start | bytes 2097152 | tf_op jit(solution)/shard_map/all_to_all | solution.py:401
  82.6 29.5 %all_gather.12 = bf16[4,2,64,512]{3,2,1,0:T(8,128)(2,1)S(1)} all-gather(bf16[1,2,64,512]{3,2,1,0:T(8,128)(2,1)S(1)} %pad_maximum_fusion.1), channel_id=1, replica_groups=mesh['island'=4,'section'=16,'fsdp'=8] {'island'}, dimensions={0}, use_global_device_ids=true | all-gather | bytes 655360 | tf_op jit(solution)/shard_map/all_gather | solution.py:407
  112.3 2.0 %fusion = f32[1,512,512]{2,1,0:T(8,128)} fusion(f32[512,256]{1,0:T(8,128)S(1)} %fusion.9, f32[64,512]{1,0:T(8,128)S(1)} %get-tuple-element.50, f32[64,512]{1,0:T(8,128)S(1)} %get-tuple-element.49, f32[64,512]{1,0:T(8,128)S(1)} %get-tuple-element.48, f32[64,512]{1,0:T(8,128)S(1)} %get-tuple-element.47), kind=kOutput, calls=%fused_computation.1 | convolution fusion | flops 403308544 | bytes 2097152 | tf_op jit(solution)/shard_map/rd,kr->dk/dot_general | solution.py:413
  115.0 1.0 copy.12
  (48 shorter events, 2.8 us)
Async XLA Ops:
  0.6 55.7 %copy-start = (f32[1,1,512,512]{3,2,1,0:T(8,128)S(1)}, f32[1,1,512,512]{3,2,1,0:T(8,128)}, u32[]{:S(2)}) copy-start(f32[1,1,512,512]{3,2,1,0:T(8,128)} %param.11) | copy-start | bytes 3145732
  0.7 4.6 %copy-start.11 = (bf16[1,1,128,512]{3,2,1,0:T(8,128)(2,1)S(1)}, bf16[1,1,128,512]{3,2,1,0:T(8,128)(2,1)}, u32[]{:S(2)}) copy-start(bf16[1,1,128,512]{3,2,1,0:T(8,128)(2,1)} %param.9) | copy-start | bytes 393220
  3.2 15.5 %copy-start.4 = (bf16[1,1,512,512]{3,2,1,0:T(8,128)(2,1)S(1)}, bf16[1,1,512,512]{3,2,1,0:T(8,128)(2,1)}, u32[]{:S(2)}) copy-start(bf16[1,1,512,512]{3,2,1,0:T(8,128)(2,1)} %param.10) | copy-start | bytes 1572868
  3.2 15.4 %collective-permute-start = (bf16[1024,512]{1,0:T(8,128)(2,1)S(1)}, bf16[1024,512]{1,0:T(8,128)(2,1)S(1)}, u32[]{:S(2)}, u32[]{:S(2)}) collective-permute-start(bf16[1024,512]{1,0:T(8,128)(2,1)S(1)} %bitcast.54), channel_id=1, source_target_pairs={{0,1},{1,0},{2,3},{3,2},{4,5},{5,4},{6,7},{7,6},{8,9},{9,8},{10,11... | collective-permute-start | bytes 3145736 | tf_op jit(solution)/shard_map/ppermute | solution.py:358
  18.7 1.6 %copy-start.2 = (bf16[1024,512]{1,0:T(8,128)(2,1)}, bf16[1024,512]{1,0:T(8,128)(2,1)S(1)}, u32[]{:S(2)}) copy-start(bf16[1024,512]{1,0:T(8,128)(2,1)S(1)} %collective-permute-done.other_ref) | copy-start | bytes 3145732
  20.2 17.1 %all-to-all-start = ((bf16[4,128,1024]{2,1,0:T(8,128)(2,1)}), bf16[4,128,1024]{2,1,0:T(8,128)(2,1)S(1)}, u32[]{:S(2)}, u32[]{:S(2)}) async-start(bf16[4,128,1024]{2,1,0:T(8,128)(2,1)} %key_back_columns.1), calls=%async_computation | async-start | bytes 2097152 | tf_op jit(solution)/shard_map/all_to_all | solution.py:362
  25.0 2.7 %copy-start.3 = (bf16[1024,512]{1,0:T(8,128)(2,1)S(1)}, bf16[1024,512]{1,0:T(8,128)(2,1)}, u32[]{:S(2)}) copy-start(bf16[1024,512]{1,0:T(8,128)(2,1)} %copy-done.2) | copy-start | bytes 3145732
  25.0 2.7 %copy-start.5 = (bf16[4,128,512]{2,1,0:T(8,128)(2,1)S(1)}, bf16[4,128,512]{2,1,0:T(8,128)(2,1)}, u32[]{:S(2)}) copy-start(bf16[4,128,512]{2,1,0:T(8,128)(2,1)} %get-tuple-element.30.own_ref) | copy-start | bytes 1572868
  25.7 11.6 %copy-start.1 = (bf16[1,1,128,4096]{3,2,1,0:T(8,128)(2,1)S(1)}, bf16[1,1,128,4096]{3,2,1,0:T(8,128)(2,1)}, u32[]{:S(2)}) copy-start(bf16[1,1,128,4096]{3,2,1,0:T(8,128)(2,1)} %param.7) | copy-start | bytes 3145732
  25.7 4.6 %collective-permute-start.1 = (bf16[4,128,256]{2,1,0:T(8,128)(2,1)S(1)}, bf16[4,128,256]{2,1,0:T(8,128)(2,1)S(1)}, u32[]{:S(2)}, u32[]{:S(2)}) collective-permute-start(bf16[4,128,256]{2,1,0:T(8,128)(2,1)S(1)} %convolution_convert_fusion.own_keys), channel_id=1, source_target_pairs={{0,1},{1,0},{2,3},{3,2},{4,5},{5,4},{6,7},{7,6},{8,9},{9,8},{10,11... | collective-permute-start | bytes 786440 | tf_op jit(solution)/shard_map/ppermute | solution.py:371
  27.8 9.5 %copy-start.9 = (f32[1,4096]{1,0:T(1,128)S(1)}, f32[1,4096]{1,0:T(1,128)}, u32[]{:S(2)}) copy-start(f32[1,4096]{1,0:T(1,128)} %gain_ref.3) | copy-start | bytes 49156
  30.3 0.7 copy-start.6
  38.9 8.2 %copy-start.14 = (bf16[2,128,512]{2,1,0:T(8,128)(2,1)S(1)}, bf16[2,128,512]{2,1,0:T(8,128)(2,1)}, u32[]{:S(2)}) copy-start(bf16[2,128,512]{2,1,0:T(8,128)(2,1)} %get-tuple-element.40) | copy-start | bytes 786436
  38.9 10.8 %copy-start.13 = (bf16[2,128,512]{2,1,0:T(8,128)(2,1)S(1)}, bf16[2,128,512]{2,1,0:T(8,128)(2,1)}, u32[]{:S(2)}) copy-start(bf16[2,128,512]{2,1,0:T(8,128)(2,1)} %get-tuple-element.41) | copy-start | bytes 786436
  39.0 14.8 %copy-start.12 = (bf16[2,128,512]{2,1,0:T(8,128)(2,1)S(1)}, bf16[2,128,512]{2,1,0:T(8,128)(2,1)}, u32[]{:S(2)}) copy-start(bf16[2,128,512]{2,1,0:T(8,128)(2,1)} %get-tuple-element.42) | copy-start | bytes 786436
  39.0 34.2 %all-to-all-start.1 = ((bf16[16,8,4096]{2,1,0:T(8,128)(2,1)}), bf16[16,8,4096]{2,1,0:T(8,128)(2,1)S(1)}, u32[]{:S(2)}, u32[]{:S(2)}) async-start(bf16[16,8,4096]{2,1,0:T(8,128)(2,1)} %branch_pieces.1), calls=%async_computation.1 | async-start | bytes 2097152 | tf_op jit(solution)/shard_map/all_to_all | solution.py:377
  47.1 15.3 %copy-start.7 = (bf16[4,128,256]{2,1,0:T(8,128)(2,1)S(1)}, bf16[4,128,256]{2,1,0:T(8,128)(2,1)}, u32[]{:S(2)}) copy-start(bf16[4,128,256]{2,1,0:T(8,128)(2,1)} %copy-done.6) | copy-start | bytes 786436
  47.1 15.3 %copy-start.8 = (bf16[2,128,512]{2,1,0:T(8,128)(2,1)S(1)}, bf16[2,128,512]{2,1,0:T(8,128)(2,1)}, u32[]{:S(2)}) copy-start(bf16[2,128,512]{2,1,0:T(8,128)(2,1)} %get-tuple-element.39.part0) | copy-start | bytes 786436
  47.1 12.8 %collective-permute-start.2 = (bf16[2,128,512]{2,1,0:T(8,128)(2,1)S(1)}, bf16[2,128,512]{2,1,0:T(8,128)(2,1)S(1)}, u32[]{:S(2)}, u32[]{:S(2)}) collective-permute-start(bf16[2,128,512]{2,1,0:T(8,128)(2,1)S(1)} %copy-done.14), channel_id=1, source_target_pairs={{0,2},{1,3},{2,4},{3,5},{4,6},{5,7},{6,0},{7,1},{8,10},{9,11},{10,... | collective-permute-start | bytes 786440 | tf_op jit(solution)/shard_map/ppermute | solution.py:381
  49.8 10.1 %collective-permute-start.3 = (bf16[2,128,512]{2,1,0:T(8,128)(2,1)S(1)}, bf16[2,128,512]{2,1,0:T(8,128)(2,1)S(1)}, u32[]{:S(2)}, u32[]{:S(2)}) collective-permute-start(bf16[2,128,512]{2,1,0:T(8,128)(2,1)S(1)} %copy-done.13), channel_id=1, source_target_pairs={{0,4},{1,5},{2,6},{3,7},{4,0},{5,1},{6,2},{7,3},{8,12},{9,13},{10,... | collective-permute-start | bytes 786440 | tf_op jit(solution)/shard_map/ppermute | solution.py:381
  53.8 8.6 %collective-permute-start.4 = (bf16[2,128,512]{2,1,0:T(8,128)(2,1)S(1)}, bf16[2,128,512]{2,1,0:T(8,128)(2,1)S(1)}, u32[]{:S(2)}, u32[]{:S(2)}) collective-permute-start(bf16[2,128,512]{2,1,0:T(8,128)(2,1)S(1)} %copy-done.12), channel_id=1, source_target_pairs={{0,6},{1,7},{2,0},{3,1},{4,2},{5,3},{6,4},{7,5},{8,14},{9,15},{10,... | collective-permute-start | bytes 786440 | tf_op jit(solution)/shard_map/ppermute | solution.py:381
  63.2 9.9 %collective-permute-start.5 = (bf16[128,512]{1,0:T(8,128)(2,1)S(1)}, bf16[128,512]{1,0:T(8,128)(2,1)S(1)}, u32[]{:S(2)}, u32[]{:S(2)}) collective-permute-start(bf16[128,512]{1,0:T(8,128)(2,1)S(1)} %pad_maximum_fusion), channel_id=1, source_target_pairs={{0,128},{128,0},{256,384},{384,256},{1,129},{129,1},{257,385},{385... | collective-permute-start | bytes 393224 | tf_op jit(solution)/shard_map/ppermute | solution.py:393
  74.3 8.3 %copy-start.10 = (f32[1,64,512]{2,1,0:T(8,128)S(1)}, f32[1,64,512]{2,1,0:T(8,128)}, u32[]{:S(2)}) copy-start(f32[1,64,512]{2,1,0:T(8,128)} %param.12) | copy-start | bytes 393220
  74.3 40.8 %all-to-all-start.2 = ((bf16[16,8,4096]{2,1,0:T(8,128)(2,1)}), bf16[16,8,4096]{2,1,0:T(8,128)(2,1)S(1)}, u32[]{:S(2)}, u32[]{:S(2)}) async-start(bf16[16,8,4096]{2,1,0:T(8,128)(2,1)} %suffix_sums.1), calls=%async_computation.2 | async-start | bytes 2097152 | tf_op jit(solution)/shard_map/all_to_all | solution.py:401
